TPU v7x, 256 devices: a whole 4x4x8 slice. The times are simulated.
256 devices in a mesh: batch: 16 (over z, core), fi: 2 (over x_lo), fj: 8 (over x_hi, y).
Axes of the slice: x: 4 (x_hi: 2, x_lo: 2; x = x_hi * 2 + x_lo), y: 4, z: 8, core: 2. Of those that a mesh axis runs over, the one named last changes fastest.
Arguments:
- student: bfloat16 [8192, 4096], P('batch', 'fi'), may hold values from -500 to 500
- teacher: bfloat16 [8192, 4096], P('batch', ('fi', 'fj')), may hold values from -500 to 500
Outputs:
- student_grad: float32 [8192, 4096], P('batch', ('fi', 'fj'))
All inputs are finite; a program needn't handle non-finite values.
Results may differ from a plain program's by a relative error of at most 0.0052.
Values may be sent and summed in bfloat16 or wider, within the bound.
No kernel may reach another device: no remote copies, remote signals or barrier semaphores. Data moves between devices by JAX's collectives and lax.ppermute only.
A program may use at most 128 MiB of HBM per device.

v0:
```python
import jax
import jax.numpy as jnp
from jax import lax
from jax.sharding import PartitionSpec as P

EPSILON = 1e-05
OFF_CROSS = 0.5
OFF_AUTO = 0.25


def standardize(values, total, square_total, clip_total):
    center = total / clip_total
    spread = square_total / clip_total - center * center
    scale = lax.rsqrt(spread + EPSILON)
    return ((values - center) * scale, scale)


def loss_blocks(block_sum, row_start, col_feature):
    width = col_feature.shape[1]
    row_feature = row_start + lax.broadcasted_iota(jnp.int32, (block_sum.shape[0], 1), 0)
    on_diagonal = row_feature == col_feature
    cross = block_sum[:, :width]
    auto = block_sum[:, width:]
    grad_cross = jnp.where(on_diagonal, 2.0 * (cross - 1.0), 2.0 * OFF_CROSS * cross).astype(
        jnp.bfloat16
    )
    grad_auto = jnp.where(on_diagonal, 0.0, 2.0 * OFF_AUTO * auto).astype(jnp.bfloat16)
    return jnp.concatenate([grad_cross, grad_auto * 2], 1)


def body(student, teacher):
    clip_local = student.shape[0]
    clip_total = clip_local * lax.axis_size("batch")
    student_wide = student.astype(jnp.float32)
    teacher_wide = teacher.astype(jnp.float32)
    totals = lax.psum(
        (
            jnp.sum(student_wide, 0),
            jnp.sum(student_wide * student_wide, 0),
            jnp.sum(teacher_wide, 0),
            jnp.sum(teacher_wide * teacher_wide, 0),
        ),
        "batch",
    )
    scaled_student, student_scale = standardize(student_wide, totals[0], totals[1], clip_total)
    scaled_teacher = standardize(teacher_wide, totals[2], totals[3], clip_total)[0]
    student_half = scaled_student.astype(jnp.bfloat16)
    teacher_half = scaled_teacher.astype(jnp.bfloat16)
    width = teacher.shape[1]
    col_index = lax.axis_index("fj")
    row_index = lax.axis_index("fi")
    batch_index = lax.axis_index("batch")
    own_slab = lax.dynamic_slice_in_dim(student_half, col_index * width, width, 1)
    teacher_cols, student_cols = (
        lax.all_gather(teacher_half, "fi", axis=1, tiled=True),
        lax.all_gather(own_slab, "fi", axis=1, tiled=True),
    )
    operands = jnp.concatenate([teacher_cols, student_cols], 1)
    block = student.shape[1]
    slice_rows = block // lax.axis_size("batch")
    swapped = lax.all_to_all(student_half, "batch", split_axis=1, concat_axis=0, tiled=True)
    left_block = swapped
    block_sum = (
        lax.dot_general(
            left_block,
            lax.all_gather(operands, "batch", axis=0, tiled=True),
            (((0,), (0,)), ((), ())),
            preferred_element_type=jnp.float32,
        )
        / clip_total
    )
    col_local = lax.broadcasted_iota(jnp.int32, (1, operands.shape[1] // 2), 1)
    col_feature = (col_local // width * lax.axis_size("fj") + col_index) * width + col_local % width
    row_start = row_index * block + batch_index * slice_rows
    loss_grad = loss_blocks(block_sum, row_start, col_feature)
    gathered = lax.all_gather(loss_grad, "batch", axis=0, tiled=True)
    left_block = gathered
    grad_rows = lax.psum_scatter(
        lax.dot_general(
            left_block, operands, (((1,), (1,)), ((), ())), preferred_element_type=jnp.float32
        ),
        "fj",
        scatter_dimension=0,
        tiled=True,
    )
    direct = grad_rows.T
    own_scaled = lax.dynamic_slice_in_dim(scaled_student, col_index * width, width, 1)
    own_scale = lax.dynamic_slice_in_dim(student_scale, col_index * width, width, 0)
    sums = lax.psum((jnp.sum(direct, 0), jnp.sum(direct * own_scaled, 0)), "batch")
    return own_scale * (direct - sums[0] / clip_total - own_scaled * (sums[1] / clip_total))


def solution(mesh):
    placed = (P("batch", "fi"), P("batch", ("fi", "fj")))
    return jax.shard_map(
        body, mesh=mesh, in_specs=placed, out_specs=P("batch", ("fi", "fj")), check_vma=False
    )
```

profile of v0, /device:TPU:1, one launch (start us, length us, event | category | flops | bytes accessed | tf_op | source)
XLA Modules:
  0.0 405.1 jit_solution(2678226351608623148)
XLA Ops:
  6.5 2.9 copy.6
  9.4 0.7 convert_reduce_fusion
  10.4 48.8 %all-reduce.1 = (f32[2048]{0:T(1024)S(1)}, f32[2048]{0:T(1024)S(1)}, f32[256]{0:T(256)S(1)}, f32[256]{0:T(256)S(1)}) all-reduce(f32[2048]{0:T(1024)S(1)} %get-tuple-element.6, f32[2048]{0:T(1024)S(1)} %get-tuple-element.5, f32[256]{0:T(256)S(1)} %get-tuple-element.8, ...), channel_id=1, replica_groups=mesh['batch'=16,'fi'=2,'fj'=8] {'batch'}, use_global_device_ids=true, to_apply=%region_1.0 | all-reduce | flops 4608 | bytes 36864 | tf_op jit(solution)/shard_map/psum | solution.py:36
  59.4 5.9 %all_gather.12 = bf16[512,512]{0,1:T(8,128)(2,1)S(1)} all-gather(bf16[512,256]{0,1:T(8,128)(2,1)S(1)} %fusion.3), channel_id=1, replica_groups=mesh['batch'=16,'fi'=2,'fj'=8] {'fi'}, dimensions={1}, use_global_device_ids=true | all-gather | bytes 786432 | tf_op jit(solution)/shard_map/all_gather | solution.py:55
  65.4 3.0 fusion.1
  68.4 1.1 constant_dynamic-slice_fusion
  69.5 5.9 %all_gather.13 = bf16[512,512]{0,1:T(8,128)(2,1)S(1)} all-gather(bf16[512,256]{0,1:T(8,128)(2,1)S(1)} %constant_dynamic-slice_fusion), channel_id=1, replica_groups=mesh['batch'=16,'fi'=2,'fj'=8] {'fi'}, dimensions={1}, use_global_device_ids=true | all-gather | bytes 786432 | tf_op jit(solution)/shard_map/all_gather | solution.py:56
  75.4 1.0 copy-done.1
  76.5 2.4 copy.7
  78.9 10.2 %all-to-all-start = ((bf16[512,16,128]{2,0,1:T(8,128)(2,1)}), bf16[512,16,128]{2,0,1:T(8,128)(2,1)S(1)}, u32[]{:S(2)}, u32[]{:S(2)}) async-start(bf16[512,16,128]{2,0,1:T(8,128)(2,1)} %copy.7), calls=%async_computation | async-start | bytes 4194304 | tf_op jit(solution)/shard_map/all_to_all | solution.py:61
  89.1 69.8 %all-to-all-done = bf16[512,16,128]{2,0,1:T(8,128)(2,1)S(1)} async-done(((bf16[512,16,128]{2,0,1:T(8,128)(2,1)}), bf16[512,16,128]{2,0,1:T(8,128)(2,1)S(1)}, u32[]{:S(2)}, u32[]{:S(2)}) %all-to-all-start) | async-done | bytes 2097184 | tf_op jit(solution)/shard_map/all_to_all | solution.py:61
  158.9 59.8 %all-gather.3.cloned.1.call-done = bf16[8192,1024]{0,1:T(8,128)(2,1)} async-done(((bf16[512,1024]{0,1:T(8,128)(2,1)}), bf16[8192,1024]{0,1:T(8,128)(2,1)}) %all-gather.3.cloned.1.call-update) | async-done | bytes 16777232 | tf_op jit(solution)/shard_map/all_gather | solution.py:66
  218.7 12.3 %convolution_multiply_fusion = f32[128,1024]{1,0:T(8,128)} fusion(bf16[8192,128]{1,0:T(8,128)(2,1)S(1)} %bitcast.18, bf16[8192,1024]{0,1:T(8,128)(2,1)} %all-gather.3.cloned.1.call-done), kind=kOutput, calls=%fused_computation.5 | convolution fusion | flops 2147614720 | bytes 19398656 | tf_op jit(solution)/shard_map/dot_general | solution.py:64
  231.0 1.0 fusion.10
  232.1 1.0 fusion.8
  233.1 0.7 pad_maximum_fusion
  233.9 41.3 %all-gather.5.cloned.1.call-done = bf16[2048,1024]{1,0:T(8,128)(2,1)} async-done(((bf16[128,1024]{1,0:T(8,128)(2,1)}), bf16[2048,1024]{1,0:T(8,128)(2,1)}) %all-gather.5.cloned.1.call-update) | async-done | bytes 4194320 | tf_op jit(solution)/shard_map/all_gather | solution.py:76
  275.2 6.5 %fusion.23 = f32[2048,512]{1,0:T(8,128)} fusion(bf16[2048,1024]{1,0:T(8,128)(2,1)} %all-gather.5.cloned.1.call-done, bf16[512,1024]{0,1:T(8,128)(2,1)S(1)} %copy-done.2), kind=kOutput, calls=%fused_computation.50 | convolution fusion | flops 2147483648 | bytes 9437184 | tf_op jit(solution)/shard_map/dot_general | solution.py:79
  281.8 86.7 %reduce-scatter.2.cloned.1.call-done = f32[256,512]{1,0:T(8,128)} async-done(((f32[2048,512]{1,0:T(8,128)}), f32[256,512]{1,0:T(8,128)}) %reduce-scatter.2.cloned.1.call-update) | async-done | bytes 524304 | tf_op jit(solution)/shard_map/reduce_scatter | solution.py:78
  368.5 1.3 fusion.7
  369.8 1.2 reduce_sum.58
  371.0 25.1 %all-reduce = (f32[256]{0:T(256)S(1)}, f32[256]{0:T(256)S(1)}) all-reduce(f32[256]{0:T(256)S(1)} %fusion.7, f32[256]{0:T(256)S(1)} %reduce_sum.58), channel_id=1, replica_groups=mesh['batch'=16,'fi'=2,'fj'=8] {'batch'}, use_global_device_ids=true, to_apply=%region_12.13 | all-reduce | flops 512 | bytes 4096 | tf_op jit(solution)/shard_map/psum | solution.py:89
  396.2 1.4 fusion.6
  397.5 1.0 copy.9
  (24 shorter events, 0.8 us)
Async XLA Ops:
  6.5 3.6 copy-start.3
  6.5 212.1 %all-gather.3.cloned.1.call-start = ((), (), s32[]{:S(2)}) async-start(), calls=%async_computation.2 | async-start | bytes 17825792 | tf_op jit(solution)/shard_map/all_gather | solution.py:66
  68.4 8.1 %copy-start = (bf16[512,2048]{0,1:T(8,128)(2,1)S(1)}, bf16[512,2048]{0,1:T(8,128)(2,1)}, u32[]{:S(2)}) copy-start(bf16[512,2048]{0,1:T(8,128)(2,1)} %get-tuple-element.16) | copy-start | bytes 6291460
  75.4 1.0 copy-start.1
  78.9 80.0 %all-to-all-start = ((bf16[512,16,128]{2,0,1:T(8,128)(2,1)}), bf16[512,16,128]{2,0,1:T(8,128)(2,1)S(1)}, u32[]{:S(2)}, u32[]{:S(2)}) async-start(bf16[512,16,128]{2,0,1:T(8,128)(2,1)} %copy.7), calls=%async_computation | async-start | bytes 4194304 | tf_op jit(solution)/shard_map/all_to_all | solution.py:61
  89.0 186.2 %all-gather.5.cloned.1.call-start = ((), (), s32[]{:S(2)}) async-start(), calls=%async_computation.3 | async-start | bytes 4456448 | tf_op jit(solution)/shard_map/all_gather | solution.py:76
  218.7 56.5 %copy-start.2 = (bf16[512,1024]{0,1:T(8,128)(2,1)S(1)}, bf16[512,1024]{0,1:T(8,128)(2,1)}, u32[]{:S(2)}) copy-start(bf16[512,1024]{0,1:T(8,128)(2,1)} %copy-done.1) | copy-start | bytes 3145732
  233.9 134.7 %reduce-scatter.2.cloned.1.call-start = ((), (), s32[]{:S(2)}) async-start(), calls=%async_computation.4 | async-start | bytes 4718592 | tf_op jit(solution)/shard_map/reduce_scatter | solution.py:78
Sparse Core Ops, SparseCore 0:
  76.6 142.0 all-gather.2
  234.0 41.1 all-gather.4
  281.8 86.6 reduce-scatter.1
where the time goes:
time: 406 us; the launch traced here: 405 us
  waiting for transfers between devices  258 us (64%)
  blocking collectives  85.8 us (21%)
  matrix products  18.8 us (5%)
  between operations  13.2 us (3%)
  other arithmetic  10.7 us (3%)
  starting transfers between devices  10.2 us (3%)
  local copies, waits for them, and re-layouts  8.71 us (2%)
    reduce_scatter x1, waiting for transfers between devices, body(): lax.psum_scatter(lax.dot_general(left_block, operands, (((1,), (1,)), (()...  86.7 us
    all_to_all x1, waiting for transfers between devices, body(): lax.all_to_all(student_half, 'batch', split_axis=1, concat_axis=0, tiled=...  69.8 us
    all_gather x1, waiting for transfers between devices, body(): lax.all_gather(operands, 'batch', axis=0, tiled=True)  59.8 us
    psum x1, blocking collectives, body(): lax.psum((jnp.sum(student_wide, 0), jnp.sum(student_wide * student_wide,...  48.8 us
    all_gather x1, waiting for transfers between devices, body(): gathered = lax.all_gather(loss_grad, 'batch', axis=0, tiled=True)  41.3 us
    psum x1, blocking collectives, body(): lax.psum((jnp.sum(direct, 0), jnp.sum(direct * own_scaled, 0)), 'batch')  25.1 us
    dot_general x1, matrix products, body(): lax.dot_general(left_block, lax.all_gather(operands, 'batch', axis=0, til...  12.3 us
    all_to_all x1, starting transfers between devices, body(): lax.all_to_all(student_half, 'batch', split_axis=1, concat_axis=0, tiled=...  10.2 us
  transfers between devices with their start and end apart: 4, of which 4 were waited for; matrix products, arithmetic and copies ran while one was open for 1% of the time, Pallas kernels for 0%

commit v1 on v0

v1 whole, which is shorter than its diff:
```python
import functools

import jax
import jax.numpy as jnp
from jax import lax
from jax.experimental import pallas as pl
from jax.experimental.pallas import tpu as pltpu
from jax.sharding import PartitionSpec as P

EPSILON = 1e-05
BF = jnp.bfloat16
F32 = jnp.float32
NZ, NC, NX, NY = 8, 2, 4, 4
BLK = 256
HALF = 128
PACK = 64
PAD = 16
PARAMS = pltpu.CompilerParams(vmem_limit_bytes=28 * 1024 * 1024)


def move(value, target):
    flat = lambda z, c, x, y: (z % NZ * NC + c) * 16 + x % 2 * 8 + x // 2 * NY + y % NY
    pairs = []
    for z in range(NZ):
        for c in range(NC):
            for x in range(NX):
                for y in range(NY):
                    to = target(z, c, x, y)
                    if to is not None:
                        pairs.append((flat(z, c, x, y), flat(*to)))
    return lax.ppermute(value, ("batch", "fi", "fj"), pairs)


def z_shift(value, step):
    return move(value, lambda z, c, x, y: (z + step, c, x, y))


def z_swap(value, bit):
    return move(value, lambda z, c, x, y: (z ^ bit, c, x, y))


def core_swap(value):
    return move(value, lambda z, c, x, y: (z, 1 - c, x, y))


def far(x):
    return (x + 3) % NX if x % 2 == 0 else (x + 1) % NX


def dot(a, b, dims):
    return lax.dot_general(a, b, (dims, ((), ())), preferred_element_type=F32)


def whole(a):
    return pl.BlockSpec(a.shape, lambda i, *p, n=a.ndim: (0,) * n)


def call(
    kernel,
    name,
    scalars,
    operands,
    in_specs,
    shapes,
    out_specs=None,
    grid=(1,),
    flops=0,
    nbytes=1 << 20,
    after=(),
):
    outs = [jax.ShapeDtypeStruct(s, d) for s, d in shapes]
    first, count = 1 + len(operands), len(after)

    def body(*refs):
        kernel(*refs[:first], *refs[first + count :])

    resident = pl.BlockSpec(memory_space=pltpu.VMEM)
    place_whole = (lambda a: resident) if grid == (1,) else whole
    specs = [place_whole(a) if s is None else s for a, s in zip(operands, in_specs)]
    return pl.pallas_call(
        body,
        grid_spec=pltpu.PrefetchScalarGridSpec(
            num_scalar_prefetch=1,
            grid=grid,
            in_specs=specs + [pl.BlockSpec(memory_space=pl.ANY)] * count,
            out_specs=out_specs or [place_whole(o) for o in outs],
        ),
        out_shape=outs,
        compiler_params=PARAMS,
        cost_estimate=pl.CostEstimate(flops=flops, bytes_accessed=nbytes, transcendentals=0),
        name=name,
    )(scalars, *operands, *after)


HIGHEST = lax.Precision.HIGHEST


def stage_kernel(place, student, distant, *refs):
    teacher, (keep, send) = refs[:NZ], refs[NZ:]
    cross = place[1] == 0
    for k in range(NZ):
        turned = lax.rem(place[3] + k, NY)
        source, column = (student, place[2] * NY + turned) if k < NY else (distant, turned)
        a = source[:, pl.ds(pl.multiple_of(column * BLK, BLK), BLK)]
        b = teacher[k][...]
        keep[k] = jnp.where(cross, b, a)
        send[k] = jnp.where(cross, a, b)


def stage(place, student, distant, teacher, after):
    operands = [student, distant, *teacher]
    return call(
        stage_kernel,
        "stage",
        place,
        operands,
        [None] * len(operands),
        [((NZ, student.shape[0], BLK), BF)] * 2,
        nbytes=8 << 20,
        after=after,
    )


def prepare_kernel(place, half, slab_0, slab_1, far_half, slabs):
    far_half[...] = half[...]
    slabs[0] = slab_0[...]
    slabs[1] = slab_1[...]


def prepare(place, student):
    clips = student.shape[0]
    tile = 128
    width = NY * BLK
    return call(
        prepare_kernel,
        "prepare",
        place,
        [student] * 3,
        [
            pl.BlockSpec((tile, width), lambda i, p: (i, 1 - p[2])),
            pl.BlockSpec((tile, BLK), lambda i, p: (i, p[2] * NY + p[3])),
            pl.BlockSpec((tile, BLK), lambda i, p: (i, (1 - p[2]) * NY + p[3])),
        ],
        [((clips, width), BF), ((2, clips, BLK), BF)],
        [
            pl.BlockSpec((tile, width), lambda i, p: (i, 0)),
            pl.BlockSpec((2, tile, BLK), lambda i, p: (0, i, 0)),
        ],
        grid=(clips // tile,),
    )


def rows_kernel(place, slabs, other_slabs, rows, means):
    clips = slabs.shape[1]
    for k in range(2):
        lines = slice(k * BLK, k * BLK + BLK)
        total = 0.0
        for part, source in enumerate((slabs, other_slabs)):
            wide = source[k].astype(F32).T
            rows[lines, part * clips : part * clips + clips] = wide.astype(BF)
            total = total + jnp.sum(wide, 1, keepdims=True)
        means[lines] = jnp.broadcast_to(total * (0.5 / clips), (BLK, BLK))
    line = lax.broadcasted_iota(jnp.int32, (PAD, 2 * clips), 0)
    rows[2 * BLK :] = jnp.where(line == 0, 1.0, 0.0).astype(BF)


def sums_kernel(place, keep, send, slabs, keep_total, send_total):
    for target, blocks in ((keep_total, keep), (send_total, send)):
        for k in range(10):
            lanes = slice(k * BLK, k * BLK + BLK)
            if k >= NZ and target is send_total:
                target[:, lanes] = keep_total[:, lanes]
                continue
            values = (blocks[k] if k < NZ else slabs[k - NZ]).astype(F32)
            target[0:1, lanes] = jnp.sum(values, 0, keepdims=True)
            target[1:2, lanes] = jnp.sum(values * values, 0, keepdims=True)


def column_sums(place, keep, send, slabs):
    operands = [keep, send, slabs]
    return call(
        sums_kernel,
        "column_sums",
        place,
        operands,
        [None] * 3,
        [((2, 10 * BLK), F32)] * 2,
        nbytes=6 << 20,
    )


def pack_kernel(place, own, other, out):
    total = own[...] + other[...]
    lines = [
        total[kind : kind + 1, n * HALF : n * HALF + HALF] for kind in range(2) for n in range(20)
    ]
    rest = jnp.concatenate(lines, 0)
    terms = []
    for _ in range(3):
        term = rest.astype(BF).astype(F32)
        terms.append(term)
        rest = rest - term
    terms.append(jnp.zeros((8, HALF), F32))
    lines = jnp.concatenate(terms, 0).astype(BF)
    out[...] = jnp.concatenate([lines[:PACK], lines[PACK:]], 1)


def unpack_kernel(place, *refs):
    packed, (sums, squares) = refs[:NZ], refs[NZ:]
    square_lines = 0.0
    for k in range(NZ):
        wide = packed[k][packed[k].shape[0] - PACK :].astype(F32)
        wide = jnp.concatenate([wide[:, :HALF], wide[:, HALF:]], 0)
        lines = wide[:40] + wide[40:80] + wide[80:120]
        for n in range(20):
            sums[k : k + 1, n * HALF : n * HALF + HALF] = lines[n : n + 1]
        square_lines = square_lines + lines[20:]
    for n in range(20):
        squares[:, n * HALF : n * HALF + HALF] = square_lines[n : n + 1]


def figures_of(sums, squares, clip_total):
    center = jnp.sum(sums, 0, keepdims=True) / clip_total
    scale = lax.rsqrt(squares / clip_total - center * center + EPSILON)
    return center, scale


def centered(rows, means, blocks, index):
    clips = blocks[0].shape[1]
    part = dot(rows[:, :clips], blocks[0][index], ((1,), (0,)))
    part = part + dot(rows[:, clips:], blocks[1][index], ((1,), (0,)))
    return part[: 2 * BLK] - means[...] * part[2 * BLK : 2 * BLK + 1]


def far_kernel(place, rows, means, own, other, packed, top, bottom):
    index = lax.rem(place[0] + 4, NZ)
    value = centered(rows, means, (own, other), index).astype(BF)
    top[:BLK] = value[:BLK]
    bottom[:BLK] = value[BLK:]
    top[BLK:] = packed[...]
    bottom[BLK:] = packed[...]


def product_kernel(offsets, place, rows, means, own, other, *outs):
    for k, out in zip(offsets, outs):
        index = lax.rem(place[0] + (k + NZ), NZ)
        out[...] = centered(rows, means, (own, other), index)


def gradient_kernel(
    clip_total, place, own, sums, squares, from_left, from_right, top, bottom
):
    z, core = place[0], place[1]
    clips = clip_total // NZ
    line = lax.broadcasted_iota(jnp.int32, (NZ, 1), 0)

    def figures(lanes):
        center, scale = figures_of(sums[:, lanes], squares[:, lanes], clip_total)
        away = sums[:, lanes] * (1.0 / clips) - center
        return away, jnp.where(line == 0, scale, 0.0), scale

    def outer(a, b):
        return lax.dot_general(
            a, b, (((0,), (0,)), ((), ())), precision=HIGHEST, preferred_element_type=F32
        )

    row_away, row_scale, _ = figures(slice(8 * BLK, 10 * BLK))
    away, scale, column_scale = figures(pl.ds(pl.multiple_of(z * BLK, BLK), BLK))
    height = 2 * BLK
    value = own[...] + from_left[:height].astype(F32) + from_right[:height].astype(F32)
    value = value + outer(row_away, away) * float(clips)
    value = value * outer(row_scale, scale) * (1.0 / clip_total)
    upper = value[:BLK]
    row = lax.broadcasted_iota(jnp.int32, (BLK, BLK), 0)
    col = lax.broadcasted_iota(jnp.int32, (BLK, BLK), 1)
    diagonal = row == col + z * BLK
    on = jnp.where(core == 0, 2.0 * (upper - 1.0), 0.0)
    upper = jnp.where(diagonal, on, upper)
    top[...] = (upper * column_scale).astype(BF)
    bottom[...] = (value[BLK:] * column_scale).astype(BF)


def reduce_rows(place, rows, means, blocks, packed):
    height = 2 * BLK
    flops = 2 * rows.shape[0] * rows.shape[1] * BLK

    def products(kernel, extra, count, shapes):
        operands = [rows, means, *blocks, *extra]
        return call(
            kernel,
            "products",
            place,
            operands,
            [None] * len(operands),
            shapes,
            flops=count * flops,
            nbytes=(2 + count) << 20,
        )

    def wide(*offsets):
        kernel = functools.partial(product_kernel, offsets)
        return products(kernel, (), len(offsets), [((height, BLK), F32)] * len(offsets))

    top, bottom = products(far_kernel, [packed], 1, [((BLK + PACK, BLK), BF)] * 2)
    from_left, from_right = z_shift(top, 1), z_shift(bottom, -1)
    gathered = [from_left, from_right]
    ahead, behind = wide(3, -3)
    own, *ready = wide(0, 2, -2, 1, -1)

    def add(part, arrived):
        return (part + arrived.astype(F32)).astype(BF)

    right = [add(ahead[:BLK], from_left[:BLK]), ahead[BLK:].astype(BF), from_left[BLK:]]
    left = [behind[:BLK].astype(BF), add(behind[BLK:], from_right[:BLK]), from_right[BLK:]]
    for hop in range(3):
        from_left = z_shift(jnp.concatenate(right, 0), 1)
        from_right = z_shift(jnp.concatenate(left, 0), -1)
        gathered += [from_left, from_right]
        if hop < 2:
            ahead, behind = ready[2 * hop : 2 * hop + 2]
            right = [add(ahead, from_left[:height]), from_left[height:]]
            left = [add(behind, from_right[:height]), from_right[height:]]
    return own, from_left, from_right, gathered[:-1]


def gradient(place, own, sums, squares, from_left, from_right, clip_total):
    operands = [own, sums, squares, from_left, from_right]
    return call(
        functools.partial(gradient_kernel, clip_total),
        "gradient",
        place,
        operands,
        [None] * 5,
        [((BLK, BLK), BF)] * 2,
    )


def direct_kernel(offsets, has_acc, last, clip_total, place, *refs):
    count = len(offsets)
    blocks, tops, bottoms = refs[:2], refs[2 : 2 + count], refs[2 + count : 2 + 2 * count]
    refs = refs[2 + 2 * count :]
    all_sums, all_squares = refs[:2]
    acc = refs[2] if has_acc else None
    outs = refs[3 if has_acc else 2 :]
    middle = blocks[0].shape[1]
    clips = 2 * middle
    ones = jnp.ones((PAD, BLK), BF)
    z, core = place[0], place[1]
    row = lax.broadcasted_iota(jnp.int32, (BLK, BLK), 0)
    col = lax.broadcasted_iota(jnp.int32, (BLK, BLK), 1)
    line = lax.broadcasted_iota(jnp.int32, (PAD, BLK), 0)
    total = [acc[:clips, h * BLK : h * BLK + BLK] if has_acc else None for h in range(2)]
    ends = [acc[clips:, h * BLK : h * BLK + BLK] if has_acc else None for h in range(2)]
    for k in range(count):
        index = lax.rem(z + (offsets[k] + NZ), NZ)
        lanes = pl.ds(pl.multiple_of(index * BLK, BLK), BLK)
        center, scale = figures_of(all_sums[:, lanes], all_squares[:, lanes], clip_total)
        unscale = 1.0 / scale
        means = jnp.zeros((PAD, BLK), F32)
        for n in range(3):
            high = center.astype(BF).astype(F32)
            means = jnp.where(line == n, high, means)
            center = center - high
        means = means.astype(BF)
        block = jnp.concatenate([blocks[0][index], blocks[1][index]], 0)
        for half in (1, 0):
            grad = tops[k][...] if half == 0 else bottoms[k][...]
            product = dot(block, grad, ((1,), (1,)))
            total[half] = product if total[half] is None else total[half] + product
            wide = grad.astype(F32) * unscale
            square = wide * wide
            if half == 0:
                diagonal = row == col + (index + core) * BLK
                square = jnp.where(diagonal, wide * (wide * 0.5 + 1.0), square)
            high = square.astype(BF)
            low = (square - high.astype(F32)).astype(BF)
            product = dot(ones, high, ((1,), (1,))) + dot(ones, low, ((1,), (1,)))
            both = jnp.where(line < 3, dot(means, grad, ((1,), (1,))), product)
            ends[half] = both if ends[half] is None else ends[half] + both
    for half in range(2):
        if last:
            mean = jnp.sum(ends[half][:3], 0, keepdims=True)
            for part in range(2):
                out = outs[2 * half + part]
                out[:middle] = total[half][part * middle : part * middle + middle] - mean
                out[middle:] = ends[half]
        else:
            outs[0][:clips, half * BLK : half * BLK + BLK] = total[half]
            outs[0][clips:, half * BLK : half * BLK + BLK] = ends[half]


def direct_part(place, blocks, sums, squares, offsets, tops, bottoms, acc, last, clip_total):
    clips = 2 * blocks[0].shape[1]
    more = [tops[k] for k in offsets] + [bottoms[k] for k in offsets] + [sums, squares]
    more += [] if acc is None else [acc]
    if last:
        shapes = [((clips // 2 + PAD, BLK), F32)] * 4
    else:
        shapes = [((clips + PAD, 2 * BLK), F32)]
    return call(
        functools.partial(direct_kernel, offsets, acc is not None, last, clip_total),
        "direct_part",
        place,
        [*blocks, *more],
        [None] * (2 + len(more)),
        shapes,
        flops=len(offsets) * 4 * clips * BLK * BLK,
        nbytes=8 << 20,
    )


def body(student, teacher):
    clips = student.shape[0]
    clip_total = clips * NZ * NC
    batch = lax.axis_index("batch")
    z, core = batch // NC, batch % NC
    fj = lax.axis_index("fj")
    x_hi, y = fj // NY, fj % NY
    place = jnp.stack([z, core, x_hi, y]).astype(jnp.int32)

    def join(mine, others):
        return jnp.concatenate([mine, others], 0)

    with jax.named_scope("operand_blocks"):

        def turn(value, k):
            return move(value, lambda z, c, x, y: (z, c, x, y - k))

        def partner(value):
            return move(value, lambda z, c, x, y: (z, c, x ^ 1, y))

        around = [teacher] + [turn(teacher, k) for k in (1, 2, 3)]
        across = partner(teacher)
        far_half, slabs = prepare(place, student)
        distant = move(far_half, lambda z, c, x, y: (z, c, far(x), y))
        other_slabs = core_swap(slabs)
        across = [across, turn(across, 1), partner(around[2]), turn(across, 3)]
        teacher_blocks = around + across

    with jax.named_scope("rows"):
        rows, means = call(
            rows_kernel,
            "rows",
            place,
            [slabs, other_slabs],
            [None] * 2,
            [((2 * BLK + PAD, 2 * clips), BF), ((2 * BLK, BLK), F32)],
        )

    with jax.named_scope("stage"):
        keep, send = stage(place, student, distant, teacher_blocks, [rows])
        blocks = keep, core_swap(send)

    with jax.named_scope("statistics"):
        own_sums, other_sums = column_sums(place, keep, send, slabs)
        (packed,) = call(
            pack_kernel,
            "pack",
            place,
            [own_sums, core_swap(other_sums)],
            [None] * 2,
            [((PACK, BLK), BF)],
        )

    with jax.named_scope("reduce"):
        own, right, left, gathered = reduce_rows(place, rows, means, blocks, packed)

    with jax.named_scope("statistics"):
        sums, squares = call(
            unpack_kernel,
            "unpack",
            place,
            [packed, *gathered],
            [None] * NZ,
            [((NZ, 10 * BLK), F32), ((1, 10 * BLK), F32)],
        )

    with jax.named_scope("gradient"):
        top, bottom = gradient(place, own, sums, squares, right, left, clip_total)

    with jax.named_scope("spread"):
        tops, bottoms = {0: top}, {0: bottom}
        for k in range(1, 5):
            tops[-k] = z_shift(tops[1 - k], 1)
            bottoms[k] = z_shift(bottoms[k - 1], -1)
            if k < 4:
                bottoms[-k] = z_shift(bottoms[1 - k], 1)
                tops[k] = z_shift(tops[k - 1], -1)
        tops[4] = tops[-4]

    with jax.named_scope("direct"):
        part = lambda offsets, acc, last: direct_part(
            place,
            blocks,
            sums,
            squares,
            offsets,
            tops,
            bottoms,
            acc,
            last,
            clip_total,
        )
        (acc,) = part((0, -1, 1), None, False)
        (acc,) = part((-2, 2, -3, 3), acc, False)
        own_0, away_0, own_1, away_1 = part((4,), acc, True)
        sent = own_1 + core_swap(away_1)
        wide = own_0 + core_swap(away_0)
        high = sent.astype(BF)
        low = (sent[clips:] - high[clips:].astype(F32)).astype(BF)
        arrived = move(join(high, low), lambda z, c, x, y: (z, c, (x + 2) % NX, y)).astype(F32)
        direct = wide[:clips] + arrived[:clips]
        product = wide[clips + 3] + arrived[clips + 3] + arrived[clips + PAD + 3]

    with jax.named_scope("student_grad"):
        lanes = slice(8 * BLK, 9 * BLK)
        center, scale = figures_of(sums[:, lanes], squares[:, lanes], clip_total)
        scaled = (slabs[0].astype(F32) - center) * scale
        return scale * (direct - scaled * product)


def solution(mesh):
    placed = (P("batch", "fi"), P("batch", ("fi", "fj")))
    return jax.shard_map(
        body, mesh=mesh, in_specs=placed, out_specs=P("batch", ("fi", "fj")), check_vma=False
    )
```

time: 406 us -> 124 us (0.31)
  waiting for transfers between devices: 258 us -> 42.6 us
  blocking collectives: 85.8 us -> 0 us
  starting transfers between devices: 10.2 us -> 59.1 us
  matrix products: 18.8 us -> 0 us
  Pallas kernels: 0 us -> 18.6 us
  between operations: 13.2 us -> 0.36 us
  other arithmetic: 10.7 us -> 1.69 us
  local copies, waits for them, and re-layouts: 8.71 us -> 1.65 us
    all_gather x2 -> x0, waiting for transfers between devices: 101 us -> none  [the longest x1 59.8 us: body(): lax.all_gather(operands, 'batch', axis=0, tiled=True)]
    reduce_scatter x1 -> x0, waiting for transfers between devices: 86.7 us -> none  [body(): lax.psum_scatter(lax.dot_general(left_block, operands, (((1,), (1,)), (()...]
    psum x2 -> x0, blocking collectives: 74 us -> none  [the longest x1 48.8 us: body(): lax.psum((jnp.sum(student_wide, 0), jnp.sum(student_wide * student_wide,...]
    all_to_all x1 -> x0, waiting for transfers between devices: 69.8 us -> none  [body(): lax.all_to_all(student_half, 'batch', split_axis=1, concat_axis=0, tiled=...]
    ppermute x0 -> x36, starting transfers between devices: none -> 59.1 us  [move(): return lax.ppermute(value, ('batch', 'fi', 'fj'), pairs)]
    ppermute x0 -> x36, waiting for transfers between devices: none -> 42.6 us  [move(): return lax.ppermute(value, ('batch', 'fi', 'fj'), pairs)]
    dot_general x2 -> x0, matrix products: 18.8 us -> none  [the longest x1 12.3 us: body(): lax.dot_general(left_block, lax.all_gather(operands, 'batch', axis=0, til...]
    pallas_call x0 -> x13, Pallas kernels: none -> 18.6 us  [call(): pl.pallas_call(body, grid_spec=pltpu.PrefetchScalarGridSpec(num_scalar_pr...]
  transfers between devices with their start and end apart: 4 -> 36, of which waited for: 4 -> 17; matrix products, arithmetic and copies ran while one was open for 1% -> 1% of each run, Pallas kernels for 0% -> 10%
where the time goes in v1:
time: 124 us
  starting transfers between devices  59.1 us (48%)
  waiting for transfers between devices  42.6 us (34%)
  Pallas kernels  18.6 us (15%)
  other arithmetic  1.69 us (1%)
  local copies, waits for them, and re-layouts  1.65 us (1%)
    ppermute x36, starting transfers between devices, move(): return lax.ppermute(value, ('batch', 'fi', 'fj'), pairs)  59.1 us
    ppermute x36, waiting for transfers between devices, move(): return lax.ppermute(value, ('batch', 'fi', 'fj'), pairs)  42.6 us
    pallas_call x13, Pallas kernels, call(): pl.pallas_call(body, grid_spec=pltpu.PrefetchScalarGridSpec(num_scalar_pr...  18.6 us
  transfers between devices with their start and end apart: 36, of which 17 were waited for; matrix products, arithmetic and copies ran while one was open for 1% of the time, Pallas kernels for 10%

profile of v1, /device:TPU:1, one launch (start us, length us, event | category | flops | bytes accessed | tf_op | source)
XLA Modules:
  0.0 123.9 jit_solution(4021106601904125169)
XLA Ops:
  2.7 3.4 %collective-permute-start = (bf16[512,1024]{1,0:T(8,128)(2,1)S(1)}, bf16[512,1024]{1,0:T(8,128)(2,1)S(1)}, u32[]{:S(2)}, u32[]{:S(2)}) collective-permute-start(bf16[512,1024]{1,0:T(8,128)(2,1)S(1)} %get-tuple-element.30), channel_id=1, source_target_pairs={{0,12},{1,13},{2,14},{3,15},{8,4},{9,5},{10,6},{11,7},{4,8},{5,9},... | collective-permute-start | bytes 3145736 | tf_op jit(solution)/shard_map/operand_blocks/ppermute | solution.py:31
  7.1 2.9 %collective-permute-start.2 = (bf16[512,256]{1,0:T(8,128)(2,1)S(1)}, bf16[512,256]{1,0:T(8,128)(2,1)S(1)}, u32[]{:S(2)}, u32[]{:S(2)}) collective-permute-start(bf16[512,256]{1,0:T(8,128)(2,1)S(1)} %copy-done.2), channel_id=1, source_target_pairs={{0,2},{1,3},{2,0},{3,1},{8,10},{9,11},{10,8},{11,9},{4,6},{5,7},{6... | collective-permute-start | bytes 786440 | tf_op jit(solution)/shard_map/operand_blocks/ppermute | solution.py:31
  10.8 4.2 %collective-permute-done.4.refs_7_ = bf16[512,256]{1,0:T(8,128)(2,1)S(1)} collective-permute-done((bf16[512,256]{1,0:T(8,128)(2,1)S(1)}, bf16[512,256]{1,0:T(8,128)(2,1)S(1)}, u32[]{:S(2)}, u32[]{:S(2)}) %collective-permute-start.4) | collective-permute-done | bytes 262176 | tf_op jit(solution)/shard_map/operand_blocks/ppermute | solution.py:31
  16.3 2.7 %collective-permute-start.5 = (bf16[512,256]{1,0:T(8,128)(2,1)S(1)}, bf16[512,256]{1,0:T(8,128)(2,1)S(1)}, u32[]{:S(2)}, u32[]{:S(2)}) collective-permute-start(bf16[512,256]{1,0:T(8,128)(2,1)S(1)} %collective-permute-done.4.refs_7_), channel_id=1, source_target_pairs={{0,3},{1,0},{2,1},{3,2},{8,11},{9,8},{10,9},{11,10},{4,7},{5,4},{6... | collective-permute-start | bytes 786440 | tf_op jit(solution)/shard_map/operand_blocks/ppermute | solution.py:31
  19.1 3.2 %collective-permute-done.1.refs_4_ = bf16[512,256]{1,0:T(8,128)(2,1)S(1)} collective-permute-done((bf16[512,256]{1,0:T(8,128)(2,1)S(1)}, bf16[512,256]{1,0:T(8,128)(2,1)S(1)}, u32[]{:S(2)}, u32[]{:S(2)}) %collective-permute-start.1) | collective-permute-done | bytes 262176 | tf_op jit(solution)/shard_map/operand_blocks/ppermute | solution.py:31
  27.9 2.2 %collective-permute-done.7.refs_10_ = bf16[512,256]{1,0:T(8,128)(2,1)S(1)} collective-permute-done((bf16[512,256]{1,0:T(8,128)(2,1)S(1)}, bf16[512,256]{1,0:T(8,128)(2,1)S(1)}, u32[]{:S(2)}, u32[]{:S(2)}) %collective-permute-start.7) | collective-permute-done | bytes 262176 | tf_op jit(solution)/shard_map/operand_blocks/ppermute | solution.py:31
  35.0 2.3 %collective-permute-done.9.refs_2_ = f32[2,2560]{1,0:T(2,128)S(1)} collective-permute-done((f32[2,2560]{1,0:T(2,128)S(1)}, f32[2,2560]{1,0:T(2,128)S(1)}, u32[]{:S(2)}, u32[]{:S(2)}) %collective-permute-start.9) | collective-permute-done | bytes 20512 | tf_op jit(solution)/shard_map/statistics/ppermute | solution.py:31
  42.1 4.2 %collective-permute-start.12 = (bf16[320,256]{1,0:T(8,128)(2,1)S(1)}, bf16[320,256]{1,0:T(8,128)(2,1)S(1)}, u32[]{:S(2)}, u32[]{:S(2)}) collective-permute-start(bf16[320,256]{1,0:T(8,128)(2,1)S(1)} %get-tuple-element.39), channel_id=1, source_target_pairs={{0,224},{1,225},{2,226},{3,227},{8,232},{9,233},{10,234},{11,235},... | collective-permute-start | bytes 491528 | tf_op jit(solution)/shard_map/reduce/ppermute | solution.py:31
  46.4 2.5 %products.5 = (f32[512,256]{1,0:T(8,128)S(1)}, f32[512,256]{1,0:T(8,128)S(1)}, f32[512,256]{1,0:T(8,128)S(1)}, f32[512,256]{1,0:T(8,128)S(1)}, f32[512,256]{1,0:T(8,128)S(1)}) custom-call(s32[4]{0:T(128)S(1)} %pad_add_fusion.refs_0_, bf16[528,1024]{1,0:T(8,128)(2,1)S(1)} %get-tuple-element.32.refs_11_.refs_1_, f32[512,256]{1,0:T(8,128)S(1)} %get-tuple-element.37.refs_2_, ...), custom_call_target="tpu_custom_call" | custom-call | flops 1384120320 | bytes 7340032 | tf_op jit(solution)/shard_map/reduce/products/pallas_call | solution.py:80
  49.6 3.5 %collective-permute-start.14 = (bf16[576,256]{1,0:T(8,128)(2,1)S(1)}, bf16[576,256]{1,0:T(8,128)(2,1)S(1)}, u32[]{:S(2)}, u32[]{:S(2)}) collective-permute-start(bf16[576,256]{1,0:T(8,128)(2,1)S(1)} %pad_maximum_fusion.1), channel_id=1, source_target_pairs={{0,224},{1,225},{2,226},{3,227},{8,232},{9,233},{10,234},{11,235},... | collective-permute-start | bytes 884744 | tf_op jit(solution)/shard_map/reduce/ppermute | solution.py:31
  53.1 4.8 %collective-permute-done.13.refs_4_ = bf16[576,256]{1,0:T(8,128)(2,1)S(1)} collective-permute-done((bf16[576,256]{1,0:T(8,128)(2,1)S(1)}, bf16[576,256]{1,0:T(8,128)(2,1)S(1)}, u32[]{:S(2)}, u32[]{:S(2)}) %collective-permute-start.13) | collective-permute-done | bytes 294944 | tf_op jit(solution)/shard_map/reduce/ppermute | solution.py:31
  58.3 3.5 %collective-permute-start.16 = (bf16[576,256]{1,0:T(8,128)(2,1)S(1)}, bf16[576,256]{1,0:T(8,128)(2,1)S(1)}, u32[]{:S(2)}, u32[]{:S(2)}) collective-permute-start(bf16[576,256]{1,0:T(8,128)(2,1)S(1)} %pad_maximum_fusion.3), channel_id=1, source_target_pairs={{0,224},{1,225},{2,226},{3,227},{8,232},{9,233},{10,234},{11,235},... | collective-permute-start | bytes 884744 | tf_op jit(solution)/shard_map/reduce/ppermute | solution.py:31
  61.8 4.3 %collective-permute-done.15.refs_6_ = bf16[576,256]{1,0:T(8,128)(2,1)S(1)} collective-permute-done((bf16[576,256]{1,0:T(8,128)(2,1)S(1)}, bf16[576,256]{1,0:T(8,128)(2,1)S(1)}, u32[]{:S(2)}, u32[]{:S(2)}) %collective-permute-start.15) | collective-permute-done | bytes 294944 | tf_op jit(solution)/shard_map/reduce/ppermute | solution.py:31
  66.4 3.1 %collective-permute-start.18 = (bf16[576,256]{1,0:T(8,128)(2,1)S(1)}, bf16[576,256]{1,0:T(8,128)(2,1)S(1)}, u32[]{:S(2)}, u32[]{:S(2)}) collective-permute-start(bf16[576,256]{1,0:T(8,128)(2,1)S(1)} %pad_maximum_fusion.5), channel_id=1, source_target_pairs={{0,224},{1,225},{2,226},{3,227},{8,232},{9,233},{10,234},{11,235},... | collective-permute-start | bytes 884744 | tf_op jit(solution)/shard_map/reduce/ppermute | solution.py:31
  69.5 3.5 %collective-permute-done.17.refs_8_.refs_4_ = bf16[576,256]{1,0:T(8,128)(2,1)S(1)} collective-permute-done((bf16[576,256]{1,0:T(8,128)(2,1)S(1)}, bf16[576,256]{1,0:T(8,128)(2,1)S(1)}, u32[]{:S(2)}, u32[]{:S(2)}) %collective-permute-start.17) | collective-permute-done | bytes 294944 | tf_op jit(solution)/shard_map/reduce/ppermute | solution.py:31
  75.4 2.7 %collective-permute-start.23 = (bf16[256,256]{1,0:T(8,128)(2,1)S(1)}, bf16[256,256]{1,0:T(8,128)(2,1)S(1)}, u32[]{:S(2)}, u32[]{:S(2)}) collective-permute-start(bf16[256,256]{1,0:T(8,128)(2,1)S(1)} %get-tuple-element.50.refs_6_), channel_id=1, source_target_pairs={{0,224},{1,225},{2,226},{3,227},{8,232},{9,233},{10,234},{11,235},... | collective-permute-start | bytes 393224 | tf_op jit(solution)/shard_map/spread/ppermute | solution.py:31
  80.4 2.7 %collective-permute-start.24 = (bf16[256,256]{1,0:T(8,128)(2,1)S(1)}, bf16[256,256]{1,0:T(8,128)(2,1)S(1)}, u32[]{:S(2)}, u32[]{:S(2)}) collective-permute-start(bf16[256,256]{1,0:T(8,128)(2,1)S(1)} %collective-permute-done.23.refs_8_), channel_id=1, source_target_pairs={{0,224},{1,225},{2,226},{3,227},{8,232},{9,233},{10,234},{11,235},... | collective-permute-start | bytes 393224 | tf_op jit(solution)/shard_map/spread/ppermute | solution.py:31
  87.3 2.7 %collective-permute-start.25 = (bf16[256,256]{1,0:T(8,128)(2,1)S(1)}, bf16[256,256]{1,0:T(8,128)(2,1)S(1)}, u32[]{:S(2)}, u32[]{:S(2)}) collective-permute-start(bf16[256,256]{1,0:T(8,128)(2,1)S(1)} %collective-permute-done.24.refs_8_), channel_id=1, source_target_pairs={{0,224},{1,225},{2,226},{3,227},{8,232},{9,233},{10,234},{11,235},... | collective-permute-start | bytes 393224 | tf_op jit(solution)/shard_map/spread/ppermute | solution.py:31
  92.2 2.1 %collective-permute-done.21.refs_5_ = bf16[256,256]{1,0:T(8,128)(2,1)S(1)} collective-permute-done((bf16[256,256]{1,0:T(8,128)(2,1)S(1)}, bf16[256,256]{1,0:T(8,128)(2,1)S(1)}, u32[]{:S(2)}, u32[]{:S(2)}) %collective-permute-start.21) | collective-permute-done | bytes 131104 | tf_op jit(solution)/shard_map/spread/ppermute | solution.py:31
  94.2 2.7 %collective-permute-start.26 = (bf16[256,256]{1,0:T(8,128)(2,1)S(1)}, bf16[256,256]{1,0:T(8,128)(2,1)S(1)}, u32[]{:S(2)}, u32[]{:S(2)}) collective-permute-start(bf16[256,256]{1,0:T(8,128)(2,1)S(1)} %collective-permute-done.25.refs_10_), channel_id=1, source_target_pairs={{0,224},{1,225},{2,226},{3,227},{8,232},{9,233},{10,234},{11,235},... | collective-permute-start | bytes 393224 | tf_op jit(solution)/shard_map/spread/ppermute | solution.py:31
  96.9 2.2 %direct_part.3.refs_13_ = f32[1040,512]{1,0:T(8,128)S(1)} custom-call(s32[4]{0:T(128)S(1)} %pad_add_fusion.refs_0_, bf16[8,512,256]{2,1,0:T(8,128)(2,1)S(1)} %get-tuple-element.33.refs_1_.refs_3_, bf16[8,512,256]{2,1,0:T(8,128)(2,1)S(1)} %collective-permute-done.10.refs_4_.refs_2_, bf16[256,256]{1,0:T(8,128)(2,1)S(1)} %get-tuple-element.49.refs_3_, ...), custom_call_target="tpu_custom_call" | custom-call | flops 805306368 | bytes 8388608 | tf_op jit(solution)/shard_map/direct/direct_part/pallas_call | solution.py:80
  99.2 2.7 %direct_part.4.refs_7_ = f32[1040,512]{1,0:T(8,128)S(1)} custom-call(s32[4]{0:T(128)S(1)} %pad_add_fusion.refs_0_, bf16[8,512,256]{2,1,0:T(8,128)(2,1)S(1)} %get-tuple-element.33.refs_1_.refs_3_, bf16[8,512,256]{2,1,0:T(8,128)(2,1)S(1)} %collective-permute-done.10.refs_4_.refs_2_, bf16[256,256]{1,0:T(8,128)(2,1)S(1)} %collective-permute-done.20.refs_3_, ...), custom_call_target="tpu_custom_call" | custom-call | flops 1073741824 | bytes 8388608 | tf_op jit(solution)/shard_map/direct/direct_part/pallas_call | solution.py:80
  103.3 8.5 %collective-permute-start.34 = (f32[528,256]{1,0:T(8,128)S(1)}, f32[528,256]{1,0:T(8,128)S(1)}, u32[]{:S(2)}, u32[]{:S(2)}) collective-permute-start(f32[528,256]{1,0:T(8,128)S(1)} %get-tuple-element.54), channel_id=1, source_target_pairs={{0,16},{1,17},{2,18},{3,19},{8,24},{9,25},{10,26},{11,27},{4,20},{... | collective-permute-start | bytes 1622024 | tf_op jit(solution)/shard_map/direct/ppermute | solution.py:31
  115.1 7.8 %collective-permute-done.35 = bf16[544,256]{1,0:T(8,128)(2,1)S(1)} collective-permute-done((bf16[544,256]{1,0:T(8,128)(2,1)S(1)}, bf16[544,256]{1,0:T(8,128)(2,1)S(1)}, u32[]{:S(2)}, u32[]{:S(2)}) %collective-permute-start.35) | collective-permute-done | bytes 278560 | tf_op jit(solution)/shard_map/direct/ppermute | solution.py:31
  (98 shorter events, 38.9 us)
Async XLA Ops:
  2.7 28.0 %collective-permute-start = (bf16[512,1024]{1,0:T(8,128)(2,1)S(1)}, bf16[512,1024]{1,0:T(8,128)(2,1)S(1)}, u32[]{:S(2)}, u32[]{:S(2)}) collective-permute-start(bf16[512,1024]{1,0:T(8,128)(2,1)S(1)} %get-tuple-element.30), channel_id=1, source_target_pairs={{0,12},{1,13},{2,14},{3,15},{8,4},{9,5},{10,6},{11,7},{4,8},{5,9},... | collective-permute-start | bytes 3145736 | tf_op jit(solution)/shard_map/operand_blocks/ppermute | solution.py:31
  6.1 17.6 %collective-permute-start.8 = (bf16[2,512,256]{2,1,0:T(8,128)(2,1)S(1)}, bf16[2,512,256]{2,1,0:T(8,128)(2,1)S(1)}, u32[]{:S(2)}, u32[]{:S(2)}) collective-permute-start(bf16[2,512,256]{2,1,0:T(8,128)(2,1)S(1)} %get-tuple-element.31.refs_1_.refs_3_), channel_id=1, source_target_pairs={{0,16},{1,17},{2,18},{3,19},{8,24},{9,25},{10,26},{11,27},{4,20},{... | collective-permute-start | bytes 1572872 | tf_op jit(solution)/shard_map/operand_blocks/ppermute | solution.py:31
  7.1 7.9 %collective-permute-start.4 = (bf16[512,256]{1,0:T(8,128)(2,1)S(1)}, bf16[512,256]{1,0:T(8,128)(2,1)S(1)}, u32[]{:S(2)}, u32[]{:S(2)}) collective-permute-start(bf16[512,256]{1,0:T(8,128)(2,1)S(1)} %copy-done.2), channel_id=1, source_target_pairs={{0,8},{1,9},{2,10},{3,11},{8,0},{9,1},{10,2},{11,3},{4,12},{5,13},... | collective-permute-start | bytes 786440 | tf_op jit(solution)/shard_map/operand_blocks/ppermute | solution.py:31
  7.1 9.2 %collective-permute-start.2 = (bf16[512,256]{1,0:T(8,128)(2,1)S(1)}, bf16[512,256]{1,0:T(8,128)(2,1)S(1)}, u32[]{:S(2)}, u32[]{:S(2)}) collective-permute-start(bf16[512,256]{1,0:T(8,128)(2,1)S(1)} %copy-done.2), channel_id=1, source_target_pairs={{0,2},{1,3},{2,0},{3,1},{8,10},{9,11},{10,8},{11,9},{4,6},{5,7},{6... | collective-permute-start | bytes 786440 | tf_op jit(solution)/shard_map/operand_blocks/ppermute | solution.py:31
  10.0 12.3 %collective-permute-start.1 = (bf16[512,256]{1,0:T(8,128)(2,1)S(1)}, bf16[512,256]{1,0:T(8,128)(2,1)S(1)}, u32[]{:S(2)}, u32[]{:S(2)}) collective-permute-start(bf16[512,256]{1,0:T(8,128)(2,1)S(1)} %copy-done.2), channel_id=1, source_target_pairs={{0,3},{1,0},{2,1},{3,2},{8,11},{9,8},{10,9},{11,10},{4,7},{5,4},{6... | collective-permute-start | bytes 786440 | tf_op jit(solution)/shard_map/operand_blocks/ppermute | solution.py:31
  15.0 11.2 %collective-permute-start.3 = (bf16[512,256]{1,0:T(8,128)(2,1)S(1)}, bf16[512,256]{1,0:T(8,128)(2,1)S(1)}, u32[]{:S(2)}, u32[]{:S(2)}) collective-permute-start(bf16[512,256]{1,0:T(8,128)(2,1)S(1)} %copy-done.2), channel_id=1, source_target_pairs={{0,1},{1,2},{2,3},{3,0},{8,9},{9,10},{10,11},{11,8},{4,5},{5,6},{6... | collective-permute-start | bytes 786440 | tf_op jit(solution)/shard_map/operand_blocks/ppermute | solution.py:31
  16.3 11.6 %collective-permute-start.5 = (bf16[512,256]{1,0:T(8,128)(2,1)S(1)}, bf16[512,256]{1,0:T(8,128)(2,1)S(1)}, u32[]{:S(2)}, u32[]{:S(2)}) collective-permute-start(bf16[512,256]{1,0:T(8,128)(2,1)S(1)} %collective-permute-done.4.refs_7_), channel_id=1, source_target_pairs={{0,3},{1,0},{2,1},{3,2},{8,11},{9,8},{10,9},{11,10},{4,7},{5,4},{6... | collective-permute-start | bytes 786440 | tf_op jit(solution)/shard_map/operand_blocks/ppermute | solution.py:31
  22.3 7.8 %collective-permute-start.7 = (bf16[512,256]{1,0:T(8,128)(2,1)S(1)}, bf16[512,256]{1,0:T(8,128)(2,1)S(1)}, u32[]{:S(2)}, u32[]{:S(2)}) collective-permute-start(bf16[512,256]{1,0:T(8,128)(2,1)S(1)} %collective-permute-done.4.refs_7_), channel_id=1, source_target_pairs={{0,1},{1,2},{2,3},{3,0},{8,9},{9,10},{10,11},{11,8},{4,5},{5,6},{6... | collective-permute-start | bytes 786440 | tf_op jit(solution)/shard_map/operand_blocks/ppermute | solution.py:31
  23.7 7.0 %collective-permute-start.6 = (bf16[512,256]{1,0:T(8,128)(2,1)S(1)}, bf16[512,256]{1,0:T(8,128)(2,1)S(1)}, u32[]{:S(2)}, u32[]{:S(2)}) collective-permute-start(bf16[512,256]{1,0:T(8,128)(2,1)S(1)} %collective-permute-done.2.refs_5_), channel_id=1, source_target_pairs={{0,8},{1,9},{2,10},{3,11},{8,0},{9,1},{10,2},{11,3},{4,12},{5,13},... | collective-permute-start | bytes 786440 | tf_op jit(solution)/shard_map/operand_blocks/ppermute | solution.py:31
  39.0 9.9 %collective-permute-start.11 = (bf16[320,256]{1,0:T(8,128)(2,1)S(1)}, bf16[320,256]{1,0:T(8,128)(2,1)S(1)}, u32[]{:S(2)}, u32[]{:S(2)}) collective-permute-start(bf16[320,256]{1,0:T(8,128)(2,1)S(1)} %get-tuple-element.38), channel_id=1, source_target_pairs={{0,32},{1,33},{2,34},{3,35},{8,40},{9,41},{10,42},{11,43},{4,36},{... | collective-permute-start | bytes 491528 | tf_op jit(solution)/shard_map/reduce/ppermute | solution.py:31
  42.1 7.4 %collective-permute-start.12 = (bf16[320,256]{1,0:T(8,128)(2,1)S(1)}, bf16[320,256]{1,0:T(8,128)(2,1)S(1)}, u32[]{:S(2)}, u32[]{:S(2)}) collective-permute-start(bf16[320,256]{1,0:T(8,128)(2,1)S(1)} %get-tuple-element.39), channel_id=1, source_target_pairs={{0,224},{1,225},{2,226},{3,227},{8,232},{9,233},{10,234},{11,235},... | collective-permute-start | bytes 491528 | tf_op jit(solution)/shard_map/reduce/ppermute | solution.py:31
  49.0 9.0 %collective-permute-start.13 = (bf16[576,256]{1,0:T(8,128)(2,1)S(1)}, bf16[576,256]{1,0:T(8,128)(2,1)S(1)}, u32[]{:S(2)}, u32[]{:S(2)}) collective-permute-start(bf16[576,256]{1,0:T(8,128)(2,1)S(1)} %pad_maximum_fusion), channel_id=1, source_target_pairs={{0,32},{1,33},{2,34},{3,35},{8,40},{9,41},{10,42},{11,43},{4,36},{... | collective-permute-start | bytes 884744 | tf_op jit(solution)/shard_map/reduce/ppermute | solution.py:31
  49.6 8.6 %collective-permute-start.14 = (bf16[576,256]{1,0:T(8,128)(2,1)S(1)}, bf16[576,256]{1,0:T(8,128)(2,1)S(1)}, u32[]{:S(2)}, u32[]{:S(2)}) collective-permute-start(bf16[576,256]{1,0:T(8,128)(2,1)S(1)} %pad_maximum_fusion.1), channel_id=1, source_target_pairs={{0,224},{1,225},{2,226},{3,227},{8,232},{9,233},{10,234},{11,235},... | collective-permute-start | bytes 884744 | tf_op jit(solution)/shard_map/reduce/ppermute | solution.py:31
  58.1 8.0 %collective-permute-start.15 = (bf16[576,256]{1,0:T(8,128)(2,1)S(1)}, bf16[576,256]{1,0:T(8,128)(2,1)S(1)}, u32[]{:S(2)}, u32[]{:S(2)}) collective-permute-start(bf16[576,256]{1,0:T(8,128)(2,1)S(1)} %pad_maximum_fusion.2), channel_id=1, source_target_pairs={{0,32},{1,33},{2,34},{3,35},{8,40},{9,41},{10,42},{11,43},{4,36},{... | collective-permute-start | bytes 884744 | tf_op jit(solution)/shard_map/reduce/ppermute | solution.py:31
  58.3 8.0 %collective-permute-start.16 = (bf16[576,256]{1,0:T(8,128)(2,1)S(1)}, bf16[576,256]{1,0:T(8,128)(2,1)S(1)}, u32[]{:S(2)}, u32[]{:S(2)}) collective-permute-start(bf16[576,256]{1,0:T(8,128)(2,1)S(1)} %pad_maximum_fusion.3), channel_id=1, source_target_pairs={{0,224},{1,225},{2,226},{3,227},{8,232},{9,233},{10,234},{11,235},... | collective-permute-start | bytes 884744 | tf_op jit(solution)/shard_map/reduce/ppermute | solution.py:31
  66.4 7.3 %collective-permute-start.18 = (bf16[576,256]{1,0:T(8,128)(2,1)S(1)}, bf16[576,256]{1,0:T(8,128)(2,1)S(1)}, u32[]{:S(2)}, u32[]{:S(2)}) collective-permute-start(bf16[576,256]{1,0:T(8,128)(2,1)S(1)} %pad_maximum_fusion.5), channel_id=1, source_target_pairs={{0,224},{1,225},{2,226},{3,227},{8,232},{9,233},{10,234},{11,235},... | collective-permute-start | bytes 884744 | tf_op jit(solution)/shard_map/reduce/ppermute | solution.py:31
  87.3 6.9 %collective-permute-start.21 = (bf16[256,256]{1,0:T(8,128)(2,1)S(1)}, bf16[256,256]{1,0:T(8,128)(2,1)S(1)}, u32[]{:S(2)}, u32[]{:S(2)}) collective-permute-start(bf16[256,256]{1,0:T(8,128)(2,1)S(1)} %collective-permute-done.20.refs_3_), channel_id=1, source_target_pairs={{0,32},{1,33},{2,34},{3,35},{8,40},{9,41},{10,42},{11,43},{4,36},{... | collective-permute-start | bytes 393224 | tf_op jit(solution)/shard_map/spread/ppermute | solution.py:31
  87.3 6.9 %collective-permute-start.25 = (bf16[256,256]{1,0:T(8,128)(2,1)S(1)}, bf16[256,256]{1,0:T(8,128)(2,1)S(1)}, u32[]{:S(2)}, u32[]{:S(2)}) collective-permute-start(bf16[256,256]{1,0:T(8,128)(2,1)S(1)} %collective-permute-done.24.refs_8_), channel_id=1, source_target_pairs={{0,224},{1,225},{2,226},{3,227},{8,232},{9,233},{10,234},{11,235},... | collective-permute-start | bytes 393224 | tf_op jit(solution)/shard_map/spread/ppermute | solution.py:31
  90.0 9.1 %collective-permute-start.29 = (bf16[256,256]{1,0:T(8,128)(2,1)S(1)}, bf16[256,256]{1,0:T(8,128)(2,1)S(1)}, u32[]{:S(2)}, u32[]{:S(2)}) collective-permute-start(bf16[256,256]{1,0:T(8,128)(2,1)S(1)} %collective-permute-done.28.refs_4_), channel_id=1, source_target_pairs={{0,224},{1,225},{2,226},{3,227},{8,232},{9,233},{10,234},{11,235},... | collective-permute-start | bytes 393224 | tf_op jit(solution)/shard_map/spread/ppermute | solution.py:31
  92.2 7.0 %collective-permute-start.32 = (bf16[256,256]{1,0:T(8,128)(2,1)S(1)}, bf16[256,256]{1,0:T(8,128)(2,1)S(1)}, u32[]{:S(2)}, u32[]{:S(2)}) collective-permute-start(bf16[256,256]{1,0:T(8,128)(2,1)S(1)} %collective-permute-done.31.refs_7_), channel_id=1, source_target_pairs={{0,32},{1,33},{2,34},{3,35},{8,40},{9,41},{10,42},{11,43},{4,36},{... | collective-permute-start | bytes 393224 | tf_op jit(solution)/shard_map/spread/ppermute | solution.py:31
  94.2 7.6 %collective-permute-start.22 = (bf16[256,256]{1,0:T(8,128)(2,1)S(1)}, bf16[256,256]{1,0:T(8,128)(2,1)S(1)}, u32[]{:S(2)}, u32[]{:S(2)}) collective-permute-start(bf16[256,256]{1,0:T(8,128)(2,1)S(1)} %collective-permute-done.21.refs_5_), channel_id=1, source_target_pairs={{0,32},{1,33},{2,34},{3,35},{8,40},{9,41},{10,42},{11,43},{4,36},{... | collective-permute-start | bytes 393224 | tf_op jit(solution)/shard_map/spread/ppermute | solution.py:31
  94.2 7.7 %collective-permute-start.26 = (bf16[256,256]{1,0:T(8,128)(2,1)S(1)}, bf16[256,256]{1,0:T(8,128)(2,1)S(1)}, u32[]{:S(2)}, u32[]{:S(2)}) collective-permute-start(bf16[256,256]{1,0:T(8,128)(2,1)S(1)} %collective-permute-done.25.refs_10_), channel_id=1, source_target_pairs={{0,224},{1,225},{2,226},{3,227},{8,232},{9,233},{10,234},{11,235},... | collective-permute-start | bytes 393224 | tf_op jit(solution)/shard_map/spread/ppermute | solution.py:31
  103.3 10.1 %collective-permute-start.34 = (f32[528,256]{1,0:T(8,128)S(1)}, f32[528,256]{1,0:T(8,128)S(1)}, u32[]{:S(2)}, u32[]{:S(2)}) collective-permute-start(f32[528,256]{1,0:T(8,128)S(1)} %get-tuple-element.54), channel_id=1, source_target_pairs={{0,16},{1,17},{2,18},{3,19},{8,24},{9,25},{10,26},{11,27},{4,20},{... | collective-permute-start | bytes 1622024 | tf_op jit(solution)/shard_map/direct/ppermute | solution.py:31
  113.5 9.5 %collective-permute-start.35 = (bf16[544,256]{1,0:T(8,128)(2,1)S(1)}, bf16[544,256]{1,0:T(8,128)(2,1)S(1)}, u32[]{:S(2)}, u32[]{:S(2)}) collective-permute-start(bf16[544,256]{1,0:T(8,128)(2,1)S(1)} %pad_maximum_fusion.6), channel_id=1, source_target_pairs={{0,4},{1,5},{2,6},{3,7},{8,12},{9,13},{10,14},{11,15},{4,0},{5,1},... | collective-permute-start | bytes 835592 | tf_op jit(solution)/shard_map/direct/ppermute | solution.py:31
  (15 other events, 103.3 us)

commit v2 on v1

v2 whole, which is shorter than its diff:
```python
import functools

import jax
import jax.numpy as jnp
from jax import lax
from jax.experimental import pallas as pl
from jax.experimental.pallas import tpu as pltpu
from jax.sharding import PartitionSpec as P

EPSILON = 1e-05
BF = jnp.bfloat16
F32 = jnp.float32
NZ, NC, NX, NY = 8, 2, 4, 4
BLK = 256
HALF = 128
PACK = 64
PAD = 16
PARAMS = pltpu.CompilerParams(vmem_limit_bytes=28 * 1024 * 1024)


def move(value, target):
    flat = lambda z, c, x, y: (z % NZ * NC + c) * 16 + x % 2 * 8 + x // 2 * NY + y % NY
    pairs = []
    for z in range(NZ):
        for c in range(NC):
            for x in range(NX):
                for y in range(NY):
                    to = target(z, c, x, y)
                    if to is not None:
                        pairs.append((flat(z, c, x, y), flat(*to)))
    return lax.ppermute(value, ("batch", "fi", "fj"), pairs)


def z_shift(value, step):
    return move(value, lambda z, c, x, y: (z + step, c, x, y))


def z_swap(value, bit):
    return move(value, lambda z, c, x, y: (z ^ bit, c, x, y))


def core_swap(value):
    return move(value, lambda z, c, x, y: (z, 1 - c, x, y))


def far(x):
    return (x + 3) % NX if x % 2 == 0 else (x + 1) % NX


def dot(a, b, dims):
    return lax.dot_general(a, b, (dims, ((), ())), preferred_element_type=F32)


def whole(a):
    return pl.BlockSpec(a.shape, lambda i, *p, n=a.ndim: (0,) * n)


def call(
    kernel,
    name,
    scalars,
    operands,
    in_specs,
    shapes,
    out_specs=None,
    grid=(1,),
    flops=0,
    nbytes=1 << 20,
    after=(),
):
    outs = [jax.ShapeDtypeStruct(s, d) for s, d in shapes]
    first, count = 1 + len(operands), len(after)

    def body(*refs):
        kernel(*refs[:first], *refs[first + count :])

    resident = pl.BlockSpec(memory_space=pltpu.VMEM)
    place_whole = (lambda a: resident) if grid == (1,) else whole
    specs = [place_whole(a) if s is None else s for a, s in zip(operands, in_specs)]
    return pl.pallas_call(
        body,
        grid_spec=pltpu.PrefetchScalarGridSpec(
            num_scalar_prefetch=1,
            grid=grid,
            in_specs=specs + [pl.BlockSpec(memory_space=pl.ANY)] * count,
            out_specs=out_specs or [place_whole(o) for o in outs],
        ),
        out_shape=outs,
        compiler_params=PARAMS,
        cost_estimate=pl.CostEstimate(flops=flops, bytes_accessed=nbytes, transcendentals=0),
        name=name,
    )(scalars, *operands, *after)


def column(place, own, step):
    hi = place[2] if own else 1 - place[2]
    return pl.ds(pl.multiple_of((hi * NY + lax.rem(place[3] + step, NY)) * BLK, BLK), BLK)


def stage_kernel(place, student, distant, rows, *refs):
    teacher, (keep, send) = refs[:NZ], refs[NZ:]
    cross = place[1] == 0
    for k in range(NZ):
        if k < NY:
            a = student[:, column(place, True, k)]
        else:
            start = lax.rem(place[3] + k, NY) * BLK
            a = distant[:, pl.ds(pl.multiple_of(start, BLK), BLK)]
        b = teacher[k][...]
        keep[k] = jnp.where(cross, b, a)
        send[k] = jnp.where(cross, a, b)
    for k in range(2):
        send[NZ + k] = rows[:, k * BLK : k * BLK + BLK]


def stage(place, student, distant, rows, teacher):
    operands = [student, distant, rows, *teacher]
    return call(
        stage_kernel,
        "stage",
        place,
        operands,
        [None] * len(operands),
        [((n, student.shape[0], BLK), BF) for n in (NZ, NZ + 2)],
        nbytes=8 << 20,
    )


def far_half_kernel(place, student, far_half):
    width = far_half.shape[1]
    lanes = pl.ds(pl.multiple_of((1 - place[2]) * width, width), width)
    far_half[...] = student[:, lanes]


def rows_kernel(place, student, rows, slab):
    slab[...] = student[:, column(place, True, 0)]
    for k in range(2):
        wide = student[:, column(place, k == 0, 0)].astype(F32).T
        rows[k * BLK : k * BLK + BLK] = wide.astype(BF)


def sums_kernel(place, keep, send, student, keep_total, send_total):
    for target, blocks in ((keep_total, keep), (send_total, send)):
        for k in range(10):
            lanes = slice(k * BLK, k * BLK + BLK)
            if k >= NZ and target is send_total:
                target[:, lanes] = keep_total[:, lanes]
                continue
            if k < NZ:
                values = blocks[k].astype(F32)
            else:
                values = student[:, column(place, k == NZ, 0)].astype(F32)
            target[0:1, lanes] = jnp.sum(values, 0, keepdims=True)
            target[1:2, lanes] = jnp.sum(values * values, 0, keepdims=True)


def column_sums(place, keep, send, student):
    operands = [keep, send, student]
    return call(
        sums_kernel,
        "column_sums",
        place,
        operands,
        [None] * 3,
        [((2, 10 * BLK), F32)] * 2,
        nbytes=6 << 20,
    )


def tall(row, lanes):
    return jnp.broadcast_to(jnp.broadcast_to(row, (8, row.shape[1])).T[:, :1], lanes)


def pack_kernel(clips, place, own, other, out, totals, means):
    total = own[...] + other[...]
    totals[...] = total
    means[...] = tall(total[:1, 8 * BLK :] * (1.0 / clips), means.shape)
    lines = [
        total[kind : kind + 1, n * HALF : n * HALF + HALF] for kind in range(2) for n in range(20)
    ]
    rest = jnp.concatenate(lines, 0)
    terms = []
    for _ in range(3):
        term = rest.astype(BF).astype(F32)
        terms.append(term)
        rest = rest - term
    terms.append(jnp.zeros((8, HALF), F32))
    lines = jnp.concatenate(terms, 0).astype(BF)
    out[...] = jnp.concatenate([lines[:PACK], lines[PACK:]], 1)


def unpack_kernel(place, *refs):
    packed, (sums, squares) = refs[:NZ], refs[NZ:]
    square_lines = 0.0
    for k in range(NZ):
        wide = packed[k][packed[k].shape[0] - PACK :].astype(F32)
        wide = jnp.concatenate([wide[:, :HALF], wide[:, HALF:]], 0)
        lines = wide[:40] + wide[40:80] + wide[80:120]
        for n in range(20):
            sums[k : k + 1, n * HALF : n * HALF + HALF] = lines[n : n + 1]
        square_lines = square_lines + lines[20:]
    for n in range(20):
        squares[:, n * HALF : n * HALF + HALF] = square_lines[n : n + 1]


def figures_of(sums, squares, clip_total):
    center = jnp.sum(sums, 0, keepdims=True) / clip_total
    scale = lax.rsqrt(squares / clip_total - center * center + EPSILON)
    return center, scale


def half_kernel(place, rows, own, out):
    for k in range(NZ):
        out[k] = dot(rows[...], own[k], ((1,), (0,)))


def centered(means, totals, halves, other, index):
    part = halves[index]
    for k in range(2):
        part = part + dot(other[NZ + k], other[index, k * BLK : k * BLK + BLK], ((1,), (0,)))
    lanes = pl.ds(pl.multiple_of(index * BLK, BLK), BLK)
    return part - means[...] * totals[0:1, lanes]


def far_kernel(place, means, totals, halves, other, packed, top, bottom):
    index = lax.rem(place[0] + 4, NZ)
    value = centered(means, totals, halves, other, index).astype(BF)
    top[:BLK] = value[:BLK]
    bottom[:BLK] = value[BLK:]
    top[BLK:] = packed[...]
    bottom[BLK:] = packed[...]


def product_kernel(offsets, place, means, totals, halves, other, *outs):
    for k, out in zip(offsets, outs):
        index = lax.rem(place[0] + (k + NZ), NZ)
        out[...] = centered(means, totals, halves, other, index)


def gradient_kernel(
    clip_total, place, own, sums, squares, from_left, from_right, top, bottom
):
    z, core = place[0], place[1]
    clips = clip_total // NZ

    def figures(lanes):
        center, scale = figures_of(sums[:, lanes], squares[:, lanes], clip_total)
        return sums[:, lanes] * (1.0 / clips) - center, scale

    row_away, row_scale = figures(slice(8 * BLK, 10 * BLK))
    away, column_scale = figures(pl.ds(pl.multiple_of(z * BLK, BLK), BLK))
    height = 2 * BLK
    value = own[...] + from_left[:height].astype(F32) + from_right[:height].astype(F32)
    row_away = row_away.T
    for k in range(NZ):
        value = value + row_away[:, k : k + 1] * (away[k : k + 1] * float(clips))
    value = value * tall(row_scale, (height, BLK)) * (column_scale * (1.0 / clip_total))
    upper = value[:BLK]
    row = lax.broadcasted_iota(jnp.int32, (BLK, BLK), 0)
    col = lax.broadcasted_iota(jnp.int32, (BLK, BLK), 1)
    diagonal = row == col + z * BLK
    on = jnp.where(core == 0, 2.0 * (upper - 1.0), 0.0)
    upper = jnp.where(diagonal, on, upper)
    top[...] = (upper * column_scale).astype(BF)
    bottom[...] = (value[BLK:] * column_scale).astype(BF)


def reduce_rows(place, rows, means, totals, blocks, packed):
    height = 2 * BLK
    flops = 2 * rows.shape[0] * rows.shape[1] * BLK
    (halves,) = call(
        half_kernel,
        "half_products",
        place,
        [rows, blocks[0]],
        [None] * 2,
        [((NZ, rows.shape[0], BLK), F32)],
        flops=NZ * flops,
        nbytes=6 << 20,
    )

    def products(kernel, extra, count, shapes):
        operands = [means, totals, halves, blocks[1], *extra]
        return call(
            kernel,
            "products",
            place,
            operands,
            [None] * len(operands),
            shapes,
            flops=count * flops,
            nbytes=(2 + count) << 20,
        )

    def wide(*offsets):
        kernel = functools.partial(product_kernel, offsets)
        return products(kernel, (), len(offsets), [((height, BLK), F32)] * len(offsets))

    top, bottom = products(far_kernel, [packed], 1, [((BLK + PACK, BLK), BF)] * 2)
    from_left, from_right = z_shift(top, 1), z_shift(bottom, -1)
    gathered = [from_left, from_right]
    ahead, behind = wide(3, -3)
    own, *ready = wide(0, 2, -2, 1, -1)

    def add(part, arrived):
        return (part + arrived.astype(F32)).astype(BF)

    right = [add(ahead[:BLK], from_left[:BLK]), ahead[BLK:].astype(BF), from_left[BLK:]]
    left = [behind[:BLK].astype(BF), add(behind[BLK:], from_right[:BLK]), from_right[BLK:]]
    for hop in range(3):
        from_left = z_shift(jnp.concatenate(right, 0), 1)
        from_right = z_shift(jnp.concatenate(left, 0), -1)
        gathered += [from_left, from_right]
        if hop < 2:
            ahead, behind = ready[2 * hop : 2 * hop + 2]
            right = [add(ahead, from_left[:height]), from_left[height:]]
            left = [add(behind, from_right[:height]), from_right[height:]]
    return own, from_left, from_right, gathered[:-1]


def gradient(place, own, sums, squares, from_left, from_right, clip_total):
    operands = [own, sums, squares, from_left, from_right]
    return call(
        functools.partial(gradient_kernel, clip_total),
        "gradient",
        place,
        operands,
        [None] * 5,
        [((BLK, BLK), BF)] * 2,
    )


def direct_kernel(offsets, halves, has_acc, last, clip_total, place, *refs):
    count = len(offsets)
    blocks, refs = refs[:2], refs[2:]
    grads = []
    for _ in halves:
        grads.append(refs[:count])
        refs = refs[count:]
    all_sums, all_squares, refs = refs[0], refs[1], refs[2:]
    acc, square_acc, outs = (refs[0], refs[1], refs[2:]) if has_acc else (None, None, refs)
    middle = blocks[0].shape[1]
    clips = 2 * middle
    z, core = place[0], place[1]
    row = lax.broadcasted_iota(jnp.int32, (BLK, BLK), 0)
    col = lax.broadcasted_iota(jnp.int32, (BLK, BLK), 1)
    line = lax.broadcasted_iota(jnp.int32, (PAD, BLK), 0)
    lanes_of = lambda half: slice(half * BLK, half * BLK + BLK)
    total = {h: acc[:, lanes_of(h)] if has_acc else 0.0 for h in halves}
    squares = {h: square_acc[:, lanes_of(h)] if has_acc else 0.0 for h in halves}
    for k in range(count):
        index = lax.rem(z + (offsets[k] + NZ), NZ)
        lanes = pl.ds(pl.multiple_of(index * BLK, BLK), BLK)
        center, scale = figures_of(all_sums[:, lanes], all_squares[:, lanes], clip_total)
        unscale = 1.0 / scale
        means = jnp.zeros((PAD, BLK), F32)
        for n in range(3):
            high = center.astype(BF).astype(F32)
            means = jnp.where(line == n, high, means)
            center = center - high
        block = jnp.concatenate([blocks[0][index], blocks[1][index], means.astype(BF)], 0)
        for half, group in zip(halves, grads):
            grad = group[k][...]
            total[half] = total[half] + dot(block, grad, ((1,), (1,)))
            wide = grad.astype(F32) * unscale
            square = wide * wide
            if half == 0:
                diagonal = row == col + (index + core) * BLK
                square = jnp.where(diagonal, wide * (wide * 0.5 + 1.0), square)
            squares[half] = squares[half] + square
    for n, half in enumerate(halves):
        if not last:
            outs[0][:, lanes_of(half)] = total[half]
            outs[1][:, lanes_of(half)] = squares[half]
            continue
        ones = jnp.ones((PAD, BLK), BF)
        high = squares[half].astype(BF)
        low = (squares[half] - high.astype(F32)).astype(BF)
        product = dot(ones, high, ((1,), (1,))) + dot(ones, low, ((1,), (1,)))
        mean = jnp.sum(total[half][clips : clips + 3], 0, keepdims=True)
        for part in range(2):
            outs[2 * n + part][:middle] = total[half][part * middle : part * middle + middle] - mean
            outs[2 * n + part][middle:] = product


def direct_part(place, blocks, sums, squares, offsets, grads, acc, last, clip_total):
    clips = 2 * blocks[0].shape[1]
    gathered = [grads[half][k] for half in grads for k in offsets]
    operands = [*blocks, *gathered, sums, squares, *(acc or [])]
    if last:
        shapes = [((clips // 2 + PAD, BLK), F32)] * 4
    else:
        shapes = [((clips + PAD, 2 * BLK), F32), ((BLK, 2 * BLK), F32)]
    halves = tuple(grads)
    return call(
        functools.partial(direct_kernel, offsets, halves, acc is not None, last, clip_total),
        "direct_part",
        place,
        operands,
        [None] * len(operands),
        shapes,
        flops=len(halves) * len(offsets) * 2 * clips * BLK * BLK,
        nbytes=2 << 20,
    )


def body(student, teacher):
    clips = student.shape[0]
    clip_total = clips * NZ * NC
    batch = lax.axis_index("batch")
    z, core = batch // NC, batch % NC
    fj = lax.axis_index("fj")
    x_hi, y = fj // NY, fj % NY
    place = jnp.stack([z, core, x_hi, y]).astype(jnp.int32)

    def join(mine, others):
        return jnp.concatenate([mine, others], 0)

    with jax.named_scope("operand_blocks"):

        def turn(value, k):
            return move(value, lambda z, c, x, y: (z, c, x, y - k))

        def partner(value):
            return move(value, lambda z, c, x, y: (z, c, x ^ 1, y))

        around = [teacher] + [turn(teacher, k) for k in (1, 2, 3)]
        across = partner(teacher)
        (far_half,) = call(
            far_half_kernel,
            "far_half",
            place,
            [student],
            [None],
            [((clips, NY * BLK), BF)],
        )
        distant = move(far_half, lambda z, c, x, y: (z, c, far(x), y))
        across = [across, turn(across, 1), partner(around[2]), turn(across, 3)]
        teacher_blocks = around + across

    with jax.named_scope("rows"):
        rows, slab = call(
            rows_kernel,
            "rows",
            place,
            [student],
            [None],
            [((2 * BLK, clips), BF), ((clips, BLK), BF)],
        )

    with jax.named_scope("stage"):
        keep, send = stage(place, student, distant, rows, teacher_blocks)
        blocks = keep, core_swap(send)

    with jax.named_scope("statistics"):
        own_sums, other_sums = column_sums(place, keep, send, student)
        packed, totals, means = call(
            functools.partial(pack_kernel, 2 * clips),
            "pack",
            place,
            [own_sums, core_swap(other_sums)],
            [None] * 2,
            [((PACK, BLK), BF), ((2, 10 * BLK), F32), ((2 * BLK, BLK), F32)],
        )

    with jax.named_scope("reduce"):
        own, right, left, gathered = reduce_rows(
            place, rows, means, totals, blocks, packed
        )

    with jax.named_scope("statistics"):
        sums, squares = call(
            unpack_kernel,
            "unpack",
            place,
            [packed, *gathered],
            [None] * NZ,
            [((NZ, 10 * BLK), F32), ((1, 10 * BLK), F32)],
        )

    with jax.named_scope("gradient"):
        top, bottom = gradient(place, own, sums, squares, right, left, clip_total)

    with jax.named_scope("spread"):
        tops, bottoms = {0: top}, {0: bottom}
        for k in range(1, 5):
            tops[-k] = z_shift(tops[1 - k], 1)
            bottoms[k] = z_shift(bottoms[k - 1], -1)
            if k < 4:
                bottoms[-k] = z_shift(bottoms[1 - k], 1)
                tops[k] = z_shift(tops[k - 1], -1)
        tops[4] = tops[-4]

    with jax.named_scope("direct"):
        part = lambda offsets, grads, acc, last: direct_part(
            place, blocks, sums, squares, offsets, grads, acc, last, clip_total
        )
        acc = part((0, -1, 1), {0: tops, 1: bottoms}, None, False)
        acc = part((-2, 2, -3, 3), {0: tops, 1: bottoms}, acc, False)
        own_1, away_1, own_0, away_0 = part((4,), {1: bottoms, 0: tops}, acc, True)
        sent = own_1 + core_swap(away_1)
        wide = own_0 + core_swap(away_0)
        high = sent.astype(BF)
        low = (sent[clips:] - high[clips:].astype(F32)).astype(BF)
        arrived = move(join(high, low), lambda z, c, x, y: (z, c, (x + 2) % NX, y)).astype(F32)
        direct = wide[:clips] + arrived[:clips]
        product = wide[clips] + arrived[clips] + arrived[clips + PAD]

    with jax.named_scope("student_grad"):
        lanes = slice(8 * BLK, 9 * BLK)
        center, scale = figures_of(sums[:, lanes], squares[:, lanes], clip_total)
        scaled = (slab.astype(F32) - center) * scale
        return scale * (direct - scaled * product)


def solution(mesh):
    placed = (P("batch", "fi"), P("batch", ("fi", "fj")))
    return jax.shard_map(
        body, mesh=mesh, in_specs=placed, out_specs=P("batch", ("fi", "fj")), check_vma=False
    )
```

time: 124 us -> 121 us (0.976)
  Pallas kernels: 18.6 us -> 16.7 us
  waiting for transfers between devices: 42.6 us -> 41.2 us
    pallas_call x13 -> x14, Pallas kernels: 18.6 us -> 16.7 us  [call(): pl.pallas_call(body, grid_spec=pltpu.PrefetchScalarGridSpec(num_scalar_pr...]
    ppermute x36 -> x35, waiting for transfers between devices: 42.6 us -> 41.2 us  [move(): return lax.ppermute(value, ('batch', 'fi', 'fj'), pairs)]
    ppermute x36 -> x35, starting transfers between devices: 59.1 us -> 59.1 us  [move(): return lax.ppermute(value, ('batch', 'fi', 'fj'), pairs)]
  transfers between devices with their start and end apart: 36 -> 35, of which waited for: 17 -> 15; matrix products, arithmetic and copies ran while one was open for 1% -> 1% of each run, Pallas kernels for 10% -> 9%
where the time goes in v2:
time: 121 us
  starting transfers between devices  59.1 us (49%)
  waiting for transfers between devices  41.2 us (34%)
  Pallas kernels  16.7 us (14%)
  other arithmetic  1.73 us (1%)
  local copies, waits for them, and re-layouts  1.65 us (1%)
    ppermute x35, starting transfers between devices, move(): return lax.ppermute(value, ('batch', 'fi', 'fj'), pairs)  59.1 us
    ppermute x35, waiting for transfers between devices, move(): return lax.ppermute(value, ('batch', 'fi', 'fj'), pairs)  41.2 us
    pallas_call x14, Pallas kernels, call(): pl.pallas_call(body, grid_spec=pltpu.PrefetchScalarGridSpec(num_scalar_pr...  16.7 us
  transfers between devices with their start and end apart: 35, of which 15 were waited for; matrix products, arithmetic and copies ran while one was open for 1% of the time, Pallas kernels for 9%

profile of v2, /device:TPU:1, one launch (start us, length us, event | category | flops | bytes accessed | tf_op | source)
XLA Modules:
  0.0 120.8 jit_solution(13459024251735742502)
XLA Ops:
  2.3 3.4 %collective-permute-start = (bf16[512,1024]{1,0:T(8,128)(2,1)S(1)}, bf16[512,1024]{1,0:T(8,128)(2,1)S(1)}, u32[]{:S(2)}, u32[]{:S(2)}) collective-permute-start(bf16[512,1024]{1,0:T(8,128)(2,1)S(1)} %far_half.1), channel_id=1, source_target_pairs={{0,12},{1,13},{2,14},{3,15},{8,4},{9,5},{10,6},{11,7},{4,8},{5,9},... | collective-permute-start | bytes 3145736 | tf_op jit(solution)/shard_map/operand_blocks/ppermute | solution.py:31
  5.7 2.9 %collective-permute-start.2 = (bf16[512,256]{1,0:T(8,128)(2,1)S(1)}, bf16[512,256]{1,0:T(8,128)(2,1)S(1)}, u32[]{:S(2)}, u32[]{:S(2)}) collective-permute-start(bf16[512,256]{1,0:T(8,128)(2,1)S(1)} %copy-done.1), channel_id=1, source_target_pairs={{0,2},{1,3},{2,0},{3,1},{8,10},{9,11},{10,8},{11,9},{4,6},{5,7},{6... | collective-permute-start | bytes 786440 | tf_op jit(solution)/shard_map/operand_blocks/ppermute | solution.py:31
  10.1 2.5 %collective-permute-done.4.refs_8_ = bf16[512,256]{1,0:T(8,128)(2,1)S(1)} collective-permute-done((bf16[512,256]{1,0:T(8,128)(2,1)S(1)}, bf16[512,256]{1,0:T(8,128)(2,1)S(1)}, u32[]{:S(2)}, u32[]{:S(2)}) %collective-permute-start.4) | collective-permute-done | bytes 262176 | tf_op jit(solution)/shard_map/operand_blocks/ppermute | solution.py:31
  12.5 2.7 %collective-permute-start.5 = (bf16[512,256]{1,0:T(8,128)(2,1)S(1)}, bf16[512,256]{1,0:T(8,128)(2,1)S(1)}, u32[]{:S(2)}, u32[]{:S(2)}) collective-permute-start(bf16[512,256]{1,0:T(8,128)(2,1)S(1)} %collective-permute-done.4.refs_8_), channel_id=1, source_target_pairs={{0,3},{1,0},{2,1},{3,2},{8,11},{9,8},{10,9},{11,10},{4,7},{5,4},{6... | collective-permute-start | bytes 786440 | tf_op jit(solution)/shard_map/operand_blocks/ppermute | solution.py:31
  15.3 5.1 %collective-permute-done.1.refs_5_ = bf16[512,256]{1,0:T(8,128)(2,1)S(1)} collective-permute-done((bf16[512,256]{1,0:T(8,128)(2,1)S(1)}, bf16[512,256]{1,0:T(8,128)(2,1)S(1)}, u32[]{:S(2)}, u32[]{:S(2)}) %collective-permute-start.1) | collective-permute-done | bytes 262176 | tf_op jit(solution)/shard_map/operand_blocks/ppermute | solution.py:31
  22.6 3.4 %collective-permute-done.5.refs_9_ = bf16[512,256]{1,0:T(8,128)(2,1)S(1)} collective-permute-done((bf16[512,256]{1,0:T(8,128)(2,1)S(1)}, bf16[512,256]{1,0:T(8,128)(2,1)S(1)}, u32[]{:S(2)}, u32[]{:S(2)}) %collective-permute-start.5) | collective-permute-done | bytes 262176 | tf_op jit(solution)/shard_map/operand_blocks/ppermute | solution.py:31
  28.5 2.6 %collective-permute-start.9 = (bf16[10,512,256]{2,1,0:T(8,128)(2,1)S(1)}, bf16[10,512,256]{2,1,0:T(8,128)(2,1)S(1)}, u32[]{:S(2)}, u32[]{:S(2)}) collective-permute-start(bf16[10,512,256]{2,1,0:T(8,128)(2,1)S(1)} %get-tuple-element.37.refs_2_), channel_id=1, source_target_pairs={{0,16},{1,17},{2,18},{3,19},{8,24},{9,25},{10,26},{11,27},{4,20},{... | collective-permute-start | bytes 7864328 | tf_op jit(solution)/shard_map/stage/ppermute | solution.py:31
  40.1 4.0 %collective-permute-start.11 = (bf16[320,256]{1,0:T(8,128)(2,1)S(1)}, bf16[320,256]{1,0:T(8,128)(2,1)S(1)}, u32[]{:S(2)}, u32[]{:S(2)}) collective-permute-start(bf16[320,256]{1,0:T(8,128)(2,1)S(1)} %get-tuple-element.44), channel_id=1, source_target_pairs={{0,224},{1,225},{2,226},{3,227},{8,232},{9,233},{10,234},{11,235},... | collective-permute-start | bytes 491528 | tf_op jit(solution)/shard_map/reduce/ppermute | solution.py:31
  47.7 3.2 %collective-permute-start.13 = (bf16[576,256]{1,0:T(8,128)(2,1)S(1)}, bf16[576,256]{1,0:T(8,128)(2,1)S(1)}, u32[]{:S(2)}, u32[]{:S(2)}) collective-permute-start(bf16[576,256]{1,0:T(8,128)(2,1)S(1)} %pad_maximum_fusion.1), channel_id=1, source_target_pairs={{0,224},{1,225},{2,226},{3,227},{8,232},{9,233},{10,234},{11,235},... | collective-permute-start | bytes 884744 | tf_op jit(solution)/shard_map/reduce/ppermute | solution.py:31
  50.9 5.6 %collective-permute-done.12.refs_4_ = bf16[576,256]{1,0:T(8,128)(2,1)S(1)} collective-permute-done((bf16[576,256]{1,0:T(8,128)(2,1)S(1)}, bf16[576,256]{1,0:T(8,128)(2,1)S(1)}, u32[]{:S(2)}, u32[]{:S(2)}) %collective-permute-start.12) | collective-permute-done | bytes 294944 | tf_op jit(solution)/shard_map/reduce/ppermute | solution.py:31
  56.7 2.8 %collective-permute-start.15 = (bf16[576,256]{1,0:T(8,128)(2,1)S(1)}, bf16[576,256]{1,0:T(8,128)(2,1)S(1)}, u32[]{:S(2)}, u32[]{:S(2)}) collective-permute-start(bf16[576,256]{1,0:T(8,128)(2,1)S(1)} %pad_maximum_fusion.3), channel_id=1, source_target_pairs={{0,224},{1,225},{2,226},{3,227},{8,232},{9,233},{10,234},{11,235},... | collective-permute-start | bytes 884744 | tf_op jit(solution)/shard_map/reduce/ppermute | solution.py:31
  59.5 5.0 %collective-permute-done.14.refs_6_ = bf16[576,256]{1,0:T(8,128)(2,1)S(1)} collective-permute-done((bf16[576,256]{1,0:T(8,128)(2,1)S(1)}, bf16[576,256]{1,0:T(8,128)(2,1)S(1)}, u32[]{:S(2)}, u32[]{:S(2)}) %collective-permute-start.14) | collective-permute-done | bytes 294944 | tf_op jit(solution)/shard_map/reduce/ppermute | solution.py:31
  64.8 2.7 %collective-permute-start.17 = (bf16[576,256]{1,0:T(8,128)(2,1)S(1)}, bf16[576,256]{1,0:T(8,128)(2,1)S(1)}, u32[]{:S(2)}, u32[]{:S(2)}) collective-permute-start(bf16[576,256]{1,0:T(8,128)(2,1)S(1)} %pad_maximum_fusion.5), channel_id=1, source_target_pairs={{0,224},{1,225},{2,226},{3,227},{8,232},{9,233},{10,234},{11,235},... | collective-permute-start | bytes 884744 | tf_op jit(solution)/shard_map/reduce/ppermute | solution.py:31
  67.6 3.9 %collective-permute-done.16.refs_8_.refs_4_ = bf16[576,256]{1,0:T(8,128)(2,1)S(1)} collective-permute-done((bf16[576,256]{1,0:T(8,128)(2,1)S(1)}, bf16[576,256]{1,0:T(8,128)(2,1)S(1)}, u32[]{:S(2)}, u32[]{:S(2)}) %collective-permute-start.16) | collective-permute-done | bytes 294944 | tf_op jit(solution)/shard_map/reduce/ppermute | solution.py:31
  73.7 2.3 %collective-permute-start.18 = (bf16[256,256]{1,0:T(8,128)(2,1)S(1)}, bf16[256,256]{1,0:T(8,128)(2,1)S(1)}, u32[]{:S(2)}, u32[]{:S(2)}) collective-permute-start(bf16[256,256]{1,0:T(8,128)(2,1)S(1)} %get-tuple-element.54.refs_6_), channel_id=1, source_target_pairs={{0,224},{1,225},{2,226},{3,227},{8,232},{9,233},{10,234},{11,235},... | collective-permute-start | bytes 393224 | tf_op jit(solution)/shard_map/spread/ppermute | solution.py:31
  76.0 2.7 %collective-permute-start.26 = (bf16[256,256]{1,0:T(8,128)(2,1)S(1)}, bf16[256,256]{1,0:T(8,128)(2,1)S(1)}, u32[]{:S(2)}, u32[]{:S(2)}) collective-permute-start(bf16[256,256]{1,0:T(8,128)(2,1)S(1)} %get-tuple-element.55.refs_3_), channel_id=1, source_target_pairs={{0,224},{1,225},{2,226},{3,227},{8,232},{9,233},{10,234},{11,235},... | collective-permute-start | bytes 393224 | tf_op jit(solution)/shard_map/spread/ppermute | solution.py:31
  78.7 2.7 %collective-permute-start.19 = (bf16[256,256]{1,0:T(8,128)(2,1)S(1)}, bf16[256,256]{1,0:T(8,128)(2,1)S(1)}, u32[]{:S(2)}, u32[]{:S(2)}) collective-permute-start(bf16[256,256]{1,0:T(8,128)(2,1)S(1)} %collective-permute-done.18.refs_8_), channel_id=1, source_target_pairs={{0,224},{1,225},{2,226},{3,227},{8,232},{9,233},{10,234},{11,235},... | collective-permute-start | bytes 393224 | tf_op jit(solution)/shard_map/spread/ppermute | solution.py:31
  81.4 2.7 %collective-permute-start.27 = (bf16[256,256]{1,0:T(8,128)(2,1)S(1)}, bf16[256,256]{1,0:T(8,128)(2,1)S(1)}, u32[]{:S(2)}, u32[]{:S(2)}) collective-permute-start(bf16[256,256]{1,0:T(8,128)(2,1)S(1)} %collective-permute-done.26.refs_5_), channel_id=1, source_target_pairs={{0,224},{1,225},{2,226},{3,227},{8,232},{9,233},{10,234},{11,235},... | collective-permute-start | bytes 393224 | tf_op jit(solution)/shard_map/spread/ppermute | solution.py:31
  84.1 3.0 %collective-permute-start.20 = (bf16[256,256]{1,0:T(8,128)(2,1)S(1)}, bf16[256,256]{1,0:T(8,128)(2,1)S(1)}, u32[]{:S(2)}, u32[]{:S(2)}) collective-permute-start(bf16[256,256]{1,0:T(8,128)(2,1)S(1)} %collective-permute-done.19.refs_8_), channel_id=1, source_target_pairs={{0,224},{1,225},{2,226},{3,227},{8,232},{9,233},{10,234},{11,235},... | collective-permute-start | bytes 393224 | tf_op jit(solution)/shard_map/spread/ppermute | solution.py:31
  87.3 3.0 %collective-permute-start.28 = (bf16[256,256]{1,0:T(8,128)(2,1)S(1)}, bf16[256,256]{1,0:T(8,128)(2,1)S(1)}, u32[]{:S(2)}, u32[]{:S(2)}) collective-permute-start(bf16[256,256]{1,0:T(8,128)(2,1)S(1)} %collective-permute-done.27.refs_4_), channel_id=1, source_target_pairs={{0,224},{1,225},{2,226},{3,227},{8,232},{9,233},{10,234},{11,235},... | collective-permute-start | bytes 393224 | tf_op jit(solution)/shard_map/spread/ppermute | solution.py:31
  90.7 2.7 %collective-permute-start.21 = (bf16[256,256]{1,0:T(8,128)(2,1)S(1)}, bf16[256,256]{1,0:T(8,128)(2,1)S(1)}, u32[]{:S(2)}, u32[]{:S(2)}) collective-permute-start(bf16[256,256]{1,0:T(8,128)(2,1)S(1)} %collective-permute-done.20.refs_10_), channel_id=1, source_target_pairs={{0,224},{1,225},{2,226},{3,227},{8,232},{9,233},{10,234},{11,235},... | collective-permute-start | bytes 393224 | tf_op jit(solution)/shard_map/spread/ppermute | solution.py:31
  96.5 1.9 %direct_part.4 = (f32[1040,512]{1,0:T(8,128)S(1)}, f32[256,512]{1,0:T(8,128)S(1)}) custom-call(s32[4]{0:T(128)S(1)} %pad_add_fusion.refs_0_, bf16[8,512,256]{2,1,0:T(8,128)(2,1)S(1)} %get-tuple-element.36.refs_1_.refs_2_, bf16[10,512,256]{2,1,0:T(8,128)(2,1)S(1)} %collective-permute-done.9.refs_4_.refs_2_, ...), custom_call_target="tpu_custom_call" | custom-call | flops 1073741824 | bytes 2097152 | tf_op jit(solution)/shard_map/direct/direct_part/pallas_call | solution.py:80
  99.9 8.8 %collective-permute-start.33 = (f32[528,256]{1,0:T(8,128)S(1)}, f32[528,256]{1,0:T(8,128)S(1)}, u32[]{:S(2)}, u32[]{:S(2)}) collective-permute-start(f32[528,256]{1,0:T(8,128)S(1)} %get-tuple-element.63), channel_id=1, source_target_pairs={{0,16},{1,17},{2,18},{3,19},{8,24},{9,25},{10,26},{11,27},{4,20},{... | collective-permute-start | bytes 1622024 | tf_op jit(solution)/shard_map/direct/ppermute | solution.py:31
  112.1 7.7 %collective-permute-done.34 = bf16[544,256]{1,0:T(8,128)(2,1)S(1)} collective-permute-done((bf16[544,256]{1,0:T(8,128)(2,1)S(1)}, bf16[544,256]{1,0:T(8,128)(2,1)S(1)}, u32[]{:S(2)}, u32[]{:S(2)}) %collective-permute-start.34) | collective-permute-done | bytes 278560 | tf_op jit(solution)/shard_map/direct/ppermute | solution.py:31
  (95 shorter events, 33.2 us)
Async XLA Ops:
  2.3 25.2 %collective-permute-start = (bf16[512,1024]{1,0:T(8,128)(2,1)S(1)}, bf16[512,1024]{1,0:T(8,128)(2,1)S(1)}, u32[]{:S(2)}, u32[]{:S(2)}) collective-permute-start(bf16[512,1024]{1,0:T(8,128)(2,1)S(1)} %far_half.1), channel_id=1, source_target_pairs={{0,12},{1,13},{2,14},{3,15},{8,4},{9,5},{10,6},{11,7},{4,8},{5,9},... | collective-permute-start | bytes 3145736 | tf_op jit(solution)/shard_map/operand_blocks/ppermute | solution.py:31
  5.7 6.9 %collective-permute-start.4 = (bf16[512,256]{1,0:T(8,128)(2,1)S(1)}, bf16[512,256]{1,0:T(8,128)(2,1)S(1)}, u32[]{:S(2)}, u32[]{:S(2)}) collective-permute-start(bf16[512,256]{1,0:T(8,128)(2,1)S(1)} %copy-done.1), channel_id=1, source_target_pairs={{0,8},{1,9},{2,10},{3,11},{8,0},{9,1},{10,2},{11,3},{4,12},{5,13},... | collective-permute-start | bytes 786440 | tf_op jit(solution)/shard_map/operand_blocks/ppermute | solution.py:31
  5.7 9.6 %collective-permute-start.2 = (bf16[512,256]{1,0:T(8,128)(2,1)S(1)}, bf16[512,256]{1,0:T(8,128)(2,1)S(1)}, u32[]{:S(2)}, u32[]{:S(2)}) collective-permute-start(bf16[512,256]{1,0:T(8,128)(2,1)S(1)} %copy-done.1), channel_id=1, source_target_pairs={{0,2},{1,3},{2,0},{3,1},{8,10},{9,11},{10,8},{11,9},{4,6},{5,7},{6... | collective-permute-start | bytes 786440 | tf_op jit(solution)/shard_map/operand_blocks/ppermute | solution.py:31
  8.6 11.8 %collective-permute-start.1 = (bf16[512,256]{1,0:T(8,128)(2,1)S(1)}, bf16[512,256]{1,0:T(8,128)(2,1)S(1)}, u32[]{:S(2)}, u32[]{:S(2)}) collective-permute-start(bf16[512,256]{1,0:T(8,128)(2,1)S(1)} %copy-done.1), channel_id=1, source_target_pairs={{0,3},{1,0},{2,1},{3,2},{8,11},{9,8},{10,9},{11,10},{4,7},{5,4},{6... | collective-permute-start | bytes 786440 | tf_op jit(solution)/shard_map/operand_blocks/ppermute | solution.py:31
  9.4 13.2 %collective-permute-start.3 = (bf16[512,256]{1,0:T(8,128)(2,1)S(1)}, bf16[512,256]{1,0:T(8,128)(2,1)S(1)}, u32[]{:S(2)}, u32[]{:S(2)}) collective-permute-start(bf16[512,256]{1,0:T(8,128)(2,1)S(1)} %copy-done.1), channel_id=1, source_target_pairs={{0,1},{1,2},{2,3},{3,0},{8,9},{9,10},{10,11},{11,8},{4,5},{5,6},{6... | collective-permute-start | bytes 786440 | tf_op jit(solution)/shard_map/operand_blocks/ppermute | solution.py:31
  12.5 13.4 %collective-permute-start.5 = (bf16[512,256]{1,0:T(8,128)(2,1)S(1)}, bf16[512,256]{1,0:T(8,128)(2,1)S(1)}, u32[]{:S(2)}, u32[]{:S(2)}) collective-permute-start(bf16[512,256]{1,0:T(8,128)(2,1)S(1)} %collective-permute-done.4.refs_8_), channel_id=1, source_target_pairs={{0,3},{1,0},{2,1},{3,2},{8,11},{9,8},{10,9},{11,10},{4,7},{5,4},{6... | collective-permute-start | bytes 786440 | tf_op jit(solution)/shard_map/operand_blocks/ppermute | solution.py:31
  15.3 10.7 %collective-permute-start.7 = (bf16[512,256]{1,0:T(8,128)(2,1)S(1)}, bf16[512,256]{1,0:T(8,128)(2,1)S(1)}, u32[]{:S(2)}, u32[]{:S(2)}) collective-permute-start(bf16[512,256]{1,0:T(8,128)(2,1)S(1)} %collective-permute-done.4.refs_8_), channel_id=1, source_target_pairs={{0,1},{1,2},{2,3},{3,0},{8,9},{9,10},{10,11},{11,8},{4,5},{5,6},{6... | collective-permute-start | bytes 786440 | tf_op jit(solution)/shard_map/operand_blocks/ppermute | solution.py:31
  28.5 8.0 %collective-permute-start.9 = (bf16[10,512,256]{2,1,0:T(8,128)(2,1)S(1)}, bf16[10,512,256]{2,1,0:T(8,128)(2,1)S(1)}, u32[]{:S(2)}, u32[]{:S(2)}) collective-permute-start(bf16[10,512,256]{2,1,0:T(8,128)(2,1)S(1)} %get-tuple-element.37.refs_2_), channel_id=1, source_target_pairs={{0,16},{1,17},{2,18},{3,19},{8,24},{9,25},{10,26},{11,27},{4,20},{... | collective-permute-start | bytes 7864328 | tf_op jit(solution)/shard_map/stage/ppermute | solution.py:31
  37.3 9.9 %collective-permute-start.10 = (bf16[320,256]{1,0:T(8,128)(2,1)S(1)}, bf16[320,256]{1,0:T(8,128)(2,1)S(1)}, u32[]{:S(2)}, u32[]{:S(2)}) collective-permute-start(bf16[320,256]{1,0:T(8,128)(2,1)S(1)} %get-tuple-element.43), channel_id=1, source_target_pairs={{0,32},{1,33},{2,34},{3,35},{8,40},{9,41},{10,42},{11,43},{4,36},{... | collective-permute-start | bytes 491528 | tf_op jit(solution)/shard_map/reduce/ppermute | solution.py:31
  40.1 7.5 %collective-permute-start.11 = (bf16[320,256]{1,0:T(8,128)(2,1)S(1)}, bf16[320,256]{1,0:T(8,128)(2,1)S(1)}, u32[]{:S(2)}, u32[]{:S(2)}) collective-permute-start(bf16[320,256]{1,0:T(8,128)(2,1)S(1)} %get-tuple-element.44), channel_id=1, source_target_pairs={{0,224},{1,225},{2,226},{3,227},{8,232},{9,233},{10,234},{11,235},... | collective-permute-start | bytes 491528 | tf_op jit(solution)/shard_map/reduce/ppermute | solution.py:31
  47.3 9.1 %collective-permute-start.12 = (bf16[576,256]{1,0:T(8,128)(2,1)S(1)}, bf16[576,256]{1,0:T(8,128)(2,1)S(1)}, u32[]{:S(2)}, u32[]{:S(2)}) collective-permute-start(bf16[576,256]{1,0:T(8,128)(2,1)S(1)} %pad_maximum_fusion), channel_id=1, source_target_pairs={{0,32},{1,33},{2,34},{3,35},{8,40},{9,41},{10,42},{11,43},{4,36},{... | collective-permute-start | bytes 884744 | tf_op jit(solution)/shard_map/reduce/ppermute | solution.py:31
  47.7 8.9 %collective-permute-start.13 = (bf16[576,256]{1,0:T(8,128)(2,1)S(1)}, bf16[576,256]{1,0:T(8,128)(2,1)S(1)}, u32[]{:S(2)}, u32[]{:S(2)}) collective-permute-start(bf16[576,256]{1,0:T(8,128)(2,1)S(1)} %pad_maximum_fusion.1), channel_id=1, source_target_pairs={{0,224},{1,225},{2,226},{3,227},{8,232},{9,233},{10,234},{11,235},... | collective-permute-start | bytes 884744 | tf_op jit(solution)/shard_map/reduce/ppermute | solution.py:31
  56.5 8.0 %collective-permute-start.14 = (bf16[576,256]{1,0:T(8,128)(2,1)S(1)}, bf16[576,256]{1,0:T(8,128)(2,1)S(1)}, u32[]{:S(2)}, u32[]{:S(2)}) collective-permute-start(bf16[576,256]{1,0:T(8,128)(2,1)S(1)} %pad_maximum_fusion.2), channel_id=1, source_target_pairs={{0,32},{1,33},{2,34},{3,35},{8,40},{9,41},{10,42},{11,43},{4,36},{... | collective-permute-start | bytes 884744 | tf_op jit(solution)/shard_map/reduce/ppermute | solution.py:31
  56.7 8.0 %collective-permute-start.15 = (bf16[576,256]{1,0:T(8,128)(2,1)S(1)}, bf16[576,256]{1,0:T(8,128)(2,1)S(1)}, u32[]{:S(2)}, u32[]{:S(2)}) collective-permute-start(bf16[576,256]{1,0:T(8,128)(2,1)S(1)} %pad_maximum_fusion.3), channel_id=1, source_target_pairs={{0,224},{1,225},{2,226},{3,227},{8,232},{9,233},{10,234},{11,235},... | collective-permute-start | bytes 884744 | tf_op jit(solution)/shard_map/reduce/ppermute | solution.py:31
  64.6 6.9 %collective-permute-start.16 = (bf16[576,256]{1,0:T(8,128)(2,1)S(1)}, bf16[576,256]{1,0:T(8,128)(2,1)S(1)}, u32[]{:S(2)}, u32[]{:S(2)}) collective-permute-start(bf16[576,256]{1,0:T(8,128)(2,1)S(1)} %pad_maximum_fusion.4), channel_id=1, source_target_pairs={{0,32},{1,33},{2,34},{3,35},{8,40},{9,41},{10,42},{11,43},{4,36},{... | collective-permute-start | bytes 884744 | tf_op jit(solution)/shard_map/reduce/ppermute | solution.py:31
  64.8 7.3 %collective-permute-start.17 = (bf16[576,256]{1,0:T(8,128)(2,1)S(1)}, bf16[576,256]{1,0:T(8,128)(2,1)S(1)}, u32[]{:S(2)}, u32[]{:S(2)}) collective-permute-start(bf16[576,256]{1,0:T(8,128)(2,1)S(1)} %pad_maximum_fusion.5), channel_id=1, source_target_pairs={{0,224},{1,225},{2,226},{3,227},{8,232},{9,233},{10,234},{11,235},... | collective-permute-start | bytes 884744 | tf_op jit(solution)/shard_map/reduce/ppermute | solution.py:31
  81.4 5.9 %collective-permute-start.23 = (bf16[256,256]{1,0:T(8,128)(2,1)S(1)}, bf16[256,256]{1,0:T(8,128)(2,1)S(1)}, u32[]{:S(2)}, u32[]{:S(2)}) collective-permute-start(bf16[256,256]{1,0:T(8,128)(2,1)S(1)} %collective-permute-done.22.refs_4_), channel_id=1, source_target_pairs={{0,32},{1,33},{2,34},{3,35},{8,40},{9,41},{10,42},{11,43},{4,36},{... | collective-permute-start | bytes 393224 | tf_op jit(solution)/shard_map/spread/ppermute | solution.py:31
  84.0 6.7 %collective-permute-start.30 = (bf16[256,256]{1,0:T(8,128)(2,1)S(1)}, bf16[256,256]{1,0:T(8,128)(2,1)S(1)}, u32[]{:S(2)}, u32[]{:S(2)}) collective-permute-start(bf16[256,256]{1,0:T(8,128)(2,1)S(1)} %collective-permute-done.29.refs_7_), channel_id=1, source_target_pairs={{0,32},{1,33},{2,34},{3,35},{8,40},{9,41},{10,42},{11,43},{4,36},{... | collective-permute-start | bytes 393224 | tf_op jit(solution)/shard_map/spread/ppermute | solution.py:31
  84.1 6.7 %collective-permute-start.20 = (bf16[256,256]{1,0:T(8,128)(2,1)S(1)}, bf16[256,256]{1,0:T(8,128)(2,1)S(1)}, u32[]{:S(2)}, u32[]{:S(2)}) collective-permute-start(bf16[256,256]{1,0:T(8,128)(2,1)S(1)} %collective-permute-done.19.refs_8_), channel_id=1, source_target_pairs={{0,224},{1,225},{2,226},{3,227},{8,232},{9,233},{10,234},{11,235},... | collective-permute-start | bytes 393224 | tf_op jit(solution)/shard_map/spread/ppermute | solution.py:31
  87.3 6.1 %collective-permute-start.24 = (bf16[256,256]{1,0:T(8,128)(2,1)S(1)}, bf16[256,256]{1,0:T(8,128)(2,1)S(1)}, u32[]{:S(2)}, u32[]{:S(2)}) collective-permute-start(bf16[256,256]{1,0:T(8,128)(2,1)S(1)} %collective-permute-done.23.refs_3_), channel_id=1, source_target_pairs={{0,32},{1,33},{2,34},{3,35},{8,40},{9,41},{10,42},{11,43},{4,36},{... | collective-permute-start | bytes 393224 | tf_op jit(solution)/shard_map/spread/ppermute | solution.py:31
  87.3 7.8 %collective-permute-start.28 = (bf16[256,256]{1,0:T(8,128)(2,1)S(1)}, bf16[256,256]{1,0:T(8,128)(2,1)S(1)}, u32[]{:S(2)}, u32[]{:S(2)}) collective-permute-start(bf16[256,256]{1,0:T(8,128)(2,1)S(1)} %collective-permute-done.27.refs_4_), channel_id=1, source_target_pairs={{0,224},{1,225},{2,226},{3,227},{8,232},{9,233},{10,234},{11,235},... | collective-permute-start | bytes 393224 | tf_op jit(solution)/shard_map/spread/ppermute | solution.py:31
  90.7 7.7 %collective-permute-start.21 = (bf16[256,256]{1,0:T(8,128)(2,1)S(1)}, bf16[256,256]{1,0:T(8,128)(2,1)S(1)}, u32[]{:S(2)}, u32[]{:S(2)}) collective-permute-start(bf16[256,256]{1,0:T(8,128)(2,1)S(1)} %collective-permute-done.20.refs_10_), channel_id=1, source_target_pairs={{0,224},{1,225},{2,226},{3,227},{8,232},{9,233},{10,234},{11,235},... | collective-permute-start | bytes 393224 | tf_op jit(solution)/shard_map/spread/ppermute | solution.py:31
  99.9 10.4 %collective-permute-start.33 = (f32[528,256]{1,0:T(8,128)S(1)}, f32[528,256]{1,0:T(8,128)S(1)}, u32[]{:S(2)}, u32[]{:S(2)}) collective-permute-start(f32[528,256]{1,0:T(8,128)S(1)} %get-tuple-element.63), channel_id=1, source_target_pairs={{0,16},{1,17},{2,18},{3,19},{8,24},{9,25},{10,26},{11,27},{4,20},{... | collective-permute-start | bytes 1622024 | tf_op jit(solution)/shard_map/direct/ppermute | solution.py:31
  110.4 9.5 %collective-permute-start.34 = (bf16[544,256]{1,0:T(8,128)(2,1)S(1)}, bf16[544,256]{1,0:T(8,128)(2,1)S(1)}, u32[]{:S(2)}, u32[]{:S(2)}) collective-permute-start(bf16[544,256]{1,0:T(8,128)(2,1)S(1)} %pad_maximum_fusion.6), channel_id=1, source_target_pairs={{0,4},{1,5},{2,6},{3,7},{8,12},{9,13},{10,14},{11,15},{4,0},{5,1},... | collective-permute-start | bytes 835592 | tf_op jit(solution)/shard_map/direct/ppermute | solution.py:31
  (13 other events, 61.0 us)

commit v3 on v2

--- a/solution.py
+++ b/solution.py
@@ -238,10 +238,12 @@
 
 
 def gradient_kernel(
-    clip_total, place, own, sums, squares, from_left, from_right, top, bottom
+    clip_total, place, own, from_left, from_right, *refs
 ):
     z, core = place[0], place[1]
     clips = clip_total // NZ
+    packed, (top, bottom, sums, squares) = refs[:NZ], refs[NZ:]
+    unpack_kernel(place, *packed, sums, squares)
 
     def figures(lanes):
         center, scale = figures_of(sums[:, lanes], squares[:, lanes], clip_total)
@@ -315,18 +317,20 @@
             ahead, behind = ready[2 * hop : 2 * hop + 2]
             right = [add(ahead, from_left[:height]), from_left[height:]]
             left = [add(behind, from_right[:height]), from_right[height:]]
+            if hop == 1:
+                left = left[:1]
     return own, from_left, from_right, gathered[:-1]
 
 
-def gradient(place, own, sums, squares, from_left, from_right, clip_total):
-    operands = [own, sums, squares, from_left, from_right]
+def gradient(place, own, from_left, from_right, packed, clip_total):
+    operands = [own, from_left, from_right, *packed]
     return call(
         functools.partial(gradient_kernel, clip_total),
         "gradient",
         place,
         operands,
-        [None] * 5,
-        [((BLK, BLK), BF)] * 2,
+        [None] * len(operands),
+        [((BLK, BLK), BF)] * 2 + [((NZ, 10 * BLK), F32), ((1, 10 * BLK), F32)],
     )
 
 
@@ -468,18 +472,10 @@
             place, rows, means, totals, blocks, packed
         )
 
-    with jax.named_scope("statistics"):
-        sums, squares = call(
-            unpack_kernel,
-            "unpack",
-            place,
-            [packed, *gathered],
-            [None] * NZ,
-            [((NZ, 10 * BLK), F32), ((1, 10 * BLK), F32)],
-        )
-
     with jax.named_scope("gradient"):
-        top, bottom = gradient(place, own, sums, squares, right, left, clip_total)
+        top, bottom, sums, squares = gradient(
+            place, own, right, left, [packed, *gathered], clip_total
+        )
 
     with jax.named_scope("spread"):
         tops, bottoms = {0: top}, {0: bottom}

time: 121 us -> 121 us (level)
    pallas_call x14 -> x13, Pallas kernels: 16.7 us -> 16.1 us  [call(): pl.pallas_call(body, grid_spec=pltpu.PrefetchScalarGridSpec(num_scalar_pr...]
  transfers between devices with their start and end apart: 35 -> 35, of which waited for: 15 -> 16; matrix products, arithmetic and copies ran while one was open for 1% -> 1% of each run, Pallas kernels for 9% -> 9%
where the time goes in v3:
time: 121 us; the launch traced here: 120 us
  starting transfers between devices  58.8 us (49%)
  waiting for transfers between devices  41.8 us (35%)
  Pallas kernels  16.1 us (13%)
  other arithmetic  1.69 us (1%)
  local copies, waits for them, and re-layouts  1.65 us (1%)
    ppermute x35, starting transfers between devices, move(): return lax.ppermute(value, ('batch', 'fi', 'fj'), pairs)  58.8 us
    ppermute x35, waiting for transfers between devices, move(): return lax.ppermute(value, ('batch', 'fi', 'fj'), pairs)  41.8 us
    pallas_call x13, Pallas kernels, call(): pl.pallas_call(body, grid_spec=pltpu.PrefetchScalarGridSpec(num_scalar_pr...  16.1 us
  transfers between devices with their start and end apart: 35, of which 16 were waited for; matrix products, arithmetic and copies ran while one was open for 1% of the time, Pallas kernels for 9%

profile of v3, /device:TPU:1, one launch (start us, length us, event | category | flops | bytes accessed | tf_op | source)
XLA Modules:
  0.0 120.5 jit_solution(4661312821682552675)
XLA Ops:
  2.3 3.4 %collective-permute-start = (bf16[512,1024]{1,0:T(8,128)(2,1)S(1)}, bf16[512,1024]{1,0:T(8,128)(2,1)S(1)}, u32[]{:S(2)}, u32[]{:S(2)}) collective-permute-start(bf16[512,1024]{1,0:T(8,128)(2,1)S(1)} %far_half.1), channel_id=1, source_target_pairs={{0,12},{1,13},{2,14},{3,15},{8,4},{9,5},{10,6},{11,7},{4,8},{5,9},... | collective-permute-start | bytes 3145736 | tf_op jit(solution)/shard_map/operand_blocks/ppermute | solution.py:31
  5.7 2.9 %collective-permute-start.2 = (bf16[512,256]{1,0:T(8,128)(2,1)S(1)}, bf16[512,256]{1,0:T(8,128)(2,1)S(1)}, u32[]{:S(2)}, u32[]{:S(2)}) collective-permute-start(bf16[512,256]{1,0:T(8,128)(2,1)S(1)} %copy-done.1), channel_id=1, source_target_pairs={{0,2},{1,3},{2,0},{3,1},{8,10},{9,11},{10,8},{11,9},{4,6},{5,7},{6... | collective-permute-start | bytes 786440 | tf_op jit(solution)/shard_map/operand_blocks/ppermute | solution.py:31
  10.1 2.5 %collective-permute-done.4.refs_8_ = bf16[512,256]{1,0:T(8,128)(2,1)S(1)} collective-permute-done((bf16[512,256]{1,0:T(8,128)(2,1)S(1)}, bf16[512,256]{1,0:T(8,128)(2,1)S(1)}, u32[]{:S(2)}, u32[]{:S(2)}) %collective-permute-start.4) | collective-permute-done | bytes 262176 | tf_op jit(solution)/shard_map/operand_blocks/ppermute | solution.py:31
  12.5 2.7 %collective-permute-start.5 = (bf16[512,256]{1,0:T(8,128)(2,1)S(1)}, bf16[512,256]{1,0:T(8,128)(2,1)S(1)}, u32[]{:S(2)}, u32[]{:S(2)}) collective-permute-start(bf16[512,256]{1,0:T(8,128)(2,1)S(1)} %collective-permute-done.4.refs_8_), channel_id=1, source_target_pairs={{0,3},{1,0},{2,1},{3,2},{8,11},{9,8},{10,9},{11,10},{4,7},{5,4},{6... | collective-permute-start | bytes 786440 | tf_op jit(solution)/shard_map/operand_blocks/ppermute | solution.py:31
  15.3 5.1 %collective-permute-done.1.refs_5_ = bf16[512,256]{1,0:T(8,128)(2,1)S(1)} collective-permute-done((bf16[512,256]{1,0:T(8,128)(2,1)S(1)}, bf16[512,256]{1,0:T(8,128)(2,1)S(1)}, u32[]{:S(2)}, u32[]{:S(2)}) %collective-permute-start.1) | collective-permute-done | bytes 262176 | tf_op jit(solution)/shard_map/operand_blocks/ppermute | solution.py:31
  22.6 3.4 %collective-permute-done.5.refs_9_ = bf16[512,256]{1,0:T(8,128)(2,1)S(1)} collective-permute-done((bf16[512,256]{1,0:T(8,128)(2,1)S(1)}, bf16[512,256]{1,0:T(8,128)(2,1)S(1)}, u32[]{:S(2)}, u32[]{:S(2)}) %collective-permute-start.5) | collective-permute-done | bytes 262176 | tf_op jit(solution)/shard_map/operand_blocks/ppermute | solution.py:31
  28.5 2.6 %collective-permute-start.9 = (bf16[10,512,256]{2,1,0:T(8,128)(2,1)S(1)}, bf16[10,512,256]{2,1,0:T(8,128)(2,1)S(1)}, u32[]{:S(2)}, u32[]{:S(2)}) collective-permute-start(bf16[10,512,256]{2,1,0:T(8,128)(2,1)S(1)} %get-tuple-element.37.refs_2_), channel_id=1, source_target_pairs={{0,16},{1,17},{2,18},{3,19},{8,24},{9,25},{10,26},{11,27},{4,20},{... | collective-permute-start | bytes 7864328 | tf_op jit(solution)/shard_map/stage/ppermute | solution.py:31
  39.0 4.0 %collective-permute-start.14 = (bf16[320,256]{1,0:T(8,128)(2,1)S(1)}, bf16[320,256]{1,0:T(8,128)(2,1)S(1)}, u32[]{:S(2)}, u32[]{:S(2)}) collective-permute-start(bf16[320,256]{1,0:T(8,128)(2,1)S(1)} %get-tuple-element.51), channel_id=1, source_target_pairs={{0,224},{1,225},{2,226},{3,227},{8,232},{9,233},{10,234},{11,235},... | collective-permute-start | bytes 491528 | tf_op jit(solution)/shard_map/reduce/ppermute | solution.py:31
  47.7 2.7 %collective-permute-start.15 = (bf16[576,256]{1,0:T(8,128)(2,1)S(1)}, bf16[576,256]{1,0:T(8,128)(2,1)S(1)}, u32[]{:S(2)}, u32[]{:S(2)}) collective-permute-start(bf16[576,256]{1,0:T(8,128)(2,1)S(1)} %pad_maximum_fusion.3), channel_id=1, source_target_pairs={{0,224},{1,225},{2,226},{3,227},{8,232},{9,233},{10,234},{11,235},... | collective-permute-start | bytes 884744 | tf_op jit(solution)/shard_map/reduce/ppermute | solution.py:31
  50.4 6.0 %collective-permute-done.11.refs_7_ = bf16[576,256]{1,0:T(8,128)(2,1)S(1)} collective-permute-done((bf16[576,256]{1,0:T(8,128)(2,1)S(1)}, bf16[576,256]{1,0:T(8,128)(2,1)S(1)}, u32[]{:S(2)}, u32[]{:S(2)}) %collective-permute-start.11) | collective-permute-done | bytes 294944 | tf_op jit(solution)/shard_map/reduce/ppermute | solution.py:31
  56.7 2.7 %collective-permute-start.16 = (bf16[576,256]{1,0:T(8,128)(2,1)S(1)}, bf16[576,256]{1,0:T(8,128)(2,1)S(1)}, u32[]{:S(2)}, u32[]{:S(2)}) collective-permute-start(bf16[576,256]{1,0:T(8,128)(2,1)S(1)} %pad_maximum_fusion.4), channel_id=1, source_target_pairs={{0,224},{1,225},{2,226},{3,227},{8,232},{9,233},{10,234},{11,235},... | collective-permute-start | bytes 884744 | tf_op jit(solution)/shard_map/reduce/ppermute | solution.py:31
  59.5 5.1 %collective-permute-done.12.refs_9_ = bf16[576,256]{1,0:T(8,128)(2,1)S(1)} collective-permute-done((bf16[576,256]{1,0:T(8,128)(2,1)S(1)}, bf16[576,256]{1,0:T(8,128)(2,1)S(1)}, u32[]{:S(2)}, u32[]{:S(2)}) %collective-permute-start.12) | collective-permute-done | bytes 294944 | tf_op jit(solution)/shard_map/reduce/ppermute | solution.py:31
  64.8 2.7 %collective-permute-start.17 = (bf16[512,256]{1,0:T(8,128)(2,1)S(1)}, bf16[512,256]{1,0:T(8,128)(2,1)S(1)}, u32[]{:S(2)}, u32[]{:S(2)}) collective-permute-start(bf16[512,256]{1,0:T(8,128)(2,1)S(1)} %add_convert_fusion), channel_id=1, source_target_pairs={{0,224},{1,225},{2,226},{3,227},{8,232},{9,233},{10,234},{11,235},... | collective-permute-start | bytes 786440 | tf_op jit(solution)/shard_map/reduce/ppermute | solution.py:31
  67.5 3.3 %collective-permute-done.17.refs_3_ = bf16[512,256]{1,0:T(8,128)(2,1)S(1)} collective-permute-done((bf16[512,256]{1,0:T(8,128)(2,1)S(1)}, bf16[512,256]{1,0:T(8,128)(2,1)S(1)}, u32[]{:S(2)}, u32[]{:S(2)}) %collective-permute-start.17) | collective-permute-done | bytes 262176 | tf_op jit(solution)/shard_map/reduce/ppermute | solution.py:31
  73.1 2.6 %collective-permute-start.18 = (bf16[256,256]{1,0:T(8,128)(2,1)S(1)}, bf16[256,256]{1,0:T(8,128)(2,1)S(1)}, u32[]{:S(2)}, u32[]{:S(2)}) collective-permute-start(bf16[256,256]{1,0:T(8,128)(2,1)S(1)} %get-tuple-element.54.refs_6_), channel_id=1, source_target_pairs={{0,224},{1,225},{2,226},{3,227},{8,232},{9,233},{10,234},{11,235},... | collective-permute-start | bytes 393224 | tf_op jit(solution)/shard_map/spread/ppermute | solution.py:31
  75.7 2.7 %collective-permute-start.26 = (bf16[256,256]{1,0:T(8,128)(2,1)S(1)}, bf16[256,256]{1,0:T(8,128)(2,1)S(1)}, u32[]{:S(2)}, u32[]{:S(2)}) collective-permute-start(bf16[256,256]{1,0:T(8,128)(2,1)S(1)} %get-tuple-element.55.refs_3_), channel_id=1, source_target_pairs={{0,224},{1,225},{2,226},{3,227},{8,232},{9,233},{10,234},{11,235},... | collective-permute-start | bytes 393224 | tf_op jit(solution)/shard_map/spread/ppermute | solution.py:31
  78.3 2.7 %collective-permute-start.19 = (bf16[256,256]{1,0:T(8,128)(2,1)S(1)}, bf16[256,256]{1,0:T(8,128)(2,1)S(1)}, u32[]{:S(2)}, u32[]{:S(2)}) collective-permute-start(bf16[256,256]{1,0:T(8,128)(2,1)S(1)} %collective-permute-done.18.refs_8_), channel_id=1, source_target_pairs={{0,224},{1,225},{2,226},{3,227},{8,232},{9,233},{10,234},{11,235},... | collective-permute-start | bytes 393224 | tf_op jit(solution)/shard_map/spread/ppermute | solution.py:31
  81.0 2.7 %collective-permute-start.27 = (bf16[256,256]{1,0:T(8,128)(2,1)S(1)}, bf16[256,256]{1,0:T(8,128)(2,1)S(1)}, u32[]{:S(2)}, u32[]{:S(2)}) collective-permute-start(bf16[256,256]{1,0:T(8,128)(2,1)S(1)} %collective-permute-done.26.refs_5_), channel_id=1, source_target_pairs={{0,224},{1,225},{2,226},{3,227},{8,232},{9,233},{10,234},{11,235},... | collective-permute-start | bytes 393224 | tf_op jit(solution)/shard_map/spread/ppermute | solution.py:31
  83.7 3.0 %collective-permute-start.20 = (bf16[256,256]{1,0:T(8,128)(2,1)S(1)}, bf16[256,256]{1,0:T(8,128)(2,1)S(1)}, u32[]{:S(2)}, u32[]{:S(2)}) collective-permute-start(bf16[256,256]{1,0:T(8,128)(2,1)S(1)} %collective-permute-done.19.refs_8_), channel_id=1, source_target_pairs={{0,224},{1,225},{2,226},{3,227},{8,232},{9,233},{10,234},{11,235},... | collective-permute-start | bytes 393224 | tf_op jit(solution)/shard_map/spread/ppermute | solution.py:31
  87.0 3.0 %collective-permute-start.28 = (bf16[256,256]{1,0:T(8,128)(2,1)S(1)}, bf16[256,256]{1,0:T(8,128)(2,1)S(1)}, u32[]{:S(2)}, u32[]{:S(2)}) collective-permute-start(bf16[256,256]{1,0:T(8,128)(2,1)S(1)} %collective-permute-done.27.refs_4_), channel_id=1, source_target_pairs={{0,224},{1,225},{2,226},{3,227},{8,232},{9,233},{10,234},{11,235},... | collective-permute-start | bytes 393224 | tf_op jit(solution)/shard_map/spread/ppermute | solution.py:31
  90.4 2.7 %collective-permute-start.21 = (bf16[256,256]{1,0:T(8,128)(2,1)S(1)}, bf16[256,256]{1,0:T(8,128)(2,1)S(1)}, u32[]{:S(2)}, u32[]{:S(2)}) collective-permute-start(bf16[256,256]{1,0:T(8,128)(2,1)S(1)} %collective-permute-done.20.refs_10_), channel_id=1, source_target_pairs={{0,224},{1,225},{2,226},{3,227},{8,232},{9,233},{10,234},{11,235},... | collective-permute-start | bytes 393224 | tf_op jit(solution)/shard_map/spread/ppermute | solution.py:31
  96.2 1.9 %direct_part.4 = (f32[1040,512]{1,0:T(8,128)S(1)}, f32[256,512]{1,0:T(8,128)S(1)}) custom-call(s32[4]{0:T(128)S(1)} %pad_add_fusion.refs_0_, bf16[8,512,256]{2,1,0:T(8,128)(2,1)S(1)} %get-tuple-element.36.refs_1_.refs_2_, bf16[10,512,256]{2,1,0:T(8,128)(2,1)S(1)} %collective-permute-done.9.refs_4_.refs_2_, ...), custom_call_target="tpu_custom_call" | custom-call | flops 1073741824 | bytes 2097152 | tf_op jit(solution)/shard_map/direct/direct_part/pallas_call | solution.py:80
  99.5 8.8 %collective-permute-start.33 = (f32[528,256]{1,0:T(8,128)S(1)}, f32[528,256]{1,0:T(8,128)S(1)}, u32[]{:S(2)}, u32[]{:S(2)}) collective-permute-start(f32[528,256]{1,0:T(8,128)S(1)} %get-tuple-element.63), channel_id=1, source_target_pairs={{0,16},{1,17},{2,18},{3,19},{8,24},{9,25},{10,26},{11,27},{4,20},{... | collective-permute-start | bytes 1622024 | tf_op jit(solution)/shard_map/direct/ppermute | solution.py:31
  111.7 7.7 %collective-permute-done.34 = bf16[544,256]{1,0:T(8,128)(2,1)S(1)} collective-permute-done((bf16[544,256]{1,0:T(8,128)(2,1)S(1)}, bf16[544,256]{1,0:T(8,128)(2,1)S(1)}, u32[]{:S(2)}, u32[]{:S(2)}) %collective-permute-start.34) | collective-permute-done | bytes 278560 | tf_op jit(solution)/shard_map/direct/ppermute | solution.py:31
  (92 shorter events, 33.2 us)
Async XLA Ops:
  2.3 25.2 %collective-permute-start = (bf16[512,1024]{1,0:T(8,128)(2,1)S(1)}, bf16[512,1024]{1,0:T(8,128)(2,1)S(1)}, u32[]{:S(2)}, u32[]{:S(2)}) collective-permute-start(bf16[512,1024]{1,0:T(8,128)(2,1)S(1)} %far_half.1), channel_id=1, source_target_pairs={{0,12},{1,13},{2,14},{3,15},{8,4},{9,5},{10,6},{11,7},{4,8},{5,9},... | collective-permute-start | bytes 3145736 | tf_op jit(solution)/shard_map/operand_blocks/ppermute | solution.py:31
  5.7 6.9 %collective-permute-start.4 = (bf16[512,256]{1,0:T(8,128)(2,1)S(1)}, bf16[512,256]{1,0:T(8,128)(2,1)S(1)}, u32[]{:S(2)}, u32[]{:S(2)}) collective-permute-start(bf16[512,256]{1,0:T(8,128)(2,1)S(1)} %copy-done.1), channel_id=1, source_target_pairs={{0,8},{1,9},{2,10},{3,11},{8,0},{9,1},{10,2},{11,3},{4,12},{5,13},... | collective-permute-start | bytes 786440 | tf_op jit(solution)/shard_map/operand_blocks/ppermute | solution.py:31
  5.7 9.6 %collective-permute-start.2 = (bf16[512,256]{1,0:T(8,128)(2,1)S(1)}, bf16[512,256]{1,0:T(8,128)(2,1)S(1)}, u32[]{:S(2)}, u32[]{:S(2)}) collective-permute-start(bf16[512,256]{1,0:T(8,128)(2,1)S(1)} %copy-done.1), channel_id=1, source_target_pairs={{0,2},{1,3},{2,0},{3,1},{8,10},{9,11},{10,8},{11,9},{4,6},{5,7},{6... | collective-permute-start | bytes 786440 | tf_op jit(solution)/shard_map/operand_blocks/ppermute | solution.py:31
  8.6 11.8 %collective-permute-start.1 = (bf16[512,256]{1,0:T(8,128)(2,1)S(1)}, bf16[512,256]{1,0:T(8,128)(2,1)S(1)}, u32[]{:S(2)}, u32[]{:S(2)}) collective-permute-start(bf16[512,256]{1,0:T(8,128)(2,1)S(1)} %copy-done.1), channel_id=1, source_target_pairs={{0,3},{1,0},{2,1},{3,2},{8,11},{9,8},{10,9},{11,10},{4,7},{5,4},{6... | collective-permute-start | bytes 786440 | tf_op jit(solution)/shard_map/operand_blocks/ppermute | solution.py:31
  9.4 13.2 %collective-permute-start.3 = (bf16[512,256]{1,0:T(8,128)(2,1)S(1)}, bf16[512,256]{1,0:T(8,128)(2,1)S(1)}, u32[]{:S(2)}, u32[]{:S(2)}) collective-permute-start(bf16[512,256]{1,0:T(8,128)(2,1)S(1)} %copy-done.1), channel_id=1, source_target_pairs={{0,1},{1,2},{2,3},{3,0},{8,9},{9,10},{10,11},{11,8},{4,5},{5,6},{6... | collective-permute-start | bytes 786440 | tf_op jit(solution)/shard_map/operand_blocks/ppermute | solution.py:31
  12.5 13.4 %collective-permute-start.5 = (bf16[512,256]{1,0:T(8,128)(2,1)S(1)}, bf16[512,256]{1,0:T(8,128)(2,1)S(1)}, u32[]{:S(2)}, u32[]{:S(2)}) collective-permute-start(bf16[512,256]{1,0:T(8,128)(2,1)S(1)} %collective-permute-done.4.refs_8_), channel_id=1, source_target_pairs={{0,3},{1,0},{2,1},{3,2},{8,11},{9,8},{10,9},{11,10},{4,7},{5,4},{6... | collective-permute-start | bytes 786440 | tf_op jit(solution)/shard_map/operand_blocks/ppermute | solution.py:31
  15.3 10.7 %collective-permute-start.7 = (bf16[512,256]{1,0:T(8,128)(2,1)S(1)}, bf16[512,256]{1,0:T(8,128)(2,1)S(1)}, u32[]{:S(2)}, u32[]{:S(2)}) collective-permute-start(bf16[512,256]{1,0:T(8,128)(2,1)S(1)} %collective-permute-done.4.refs_8_), channel_id=1, source_target_pairs={{0,1},{1,2},{2,3},{3,0},{8,9},{9,10},{10,11},{11,8},{4,5},{5,6},{6... | collective-permute-start | bytes 786440 | tf_op jit(solution)/shard_map/operand_blocks/ppermute | solution.py:31
  28.5 8.0 %collective-permute-start.9 = (bf16[10,512,256]{2,1,0:T(8,128)(2,1)S(1)}, bf16[10,512,256]{2,1,0:T(8,128)(2,1)S(1)}, u32[]{:S(2)}, u32[]{:S(2)}) collective-permute-start(bf16[10,512,256]{2,1,0:T(8,128)(2,1)S(1)} %get-tuple-element.37.refs_2_), channel_id=1, source_target_pairs={{0,16},{1,17},{2,18},{3,19},{8,24},{9,25},{10,26},{11,27},{4,20},{... | collective-permute-start | bytes 7864328 | tf_op jit(solution)/shard_map/stage/ppermute | solution.py:31
  37.3 9.9 %collective-permute-start.10 = (bf16[320,256]{1,0:T(8,128)(2,1)S(1)}, bf16[320,256]{1,0:T(8,128)(2,1)S(1)}, u32[]{:S(2)}, u32[]{:S(2)}) collective-permute-start(bf16[320,256]{1,0:T(8,128)(2,1)S(1)} %get-tuple-element.47), channel_id=1, source_target_pairs={{0,32},{1,33},{2,34},{3,35},{8,40},{9,41},{10,42},{11,43},{4,36},{... | collective-permute-start | bytes 491528 | tf_op jit(solution)/shard_map/reduce/ppermute | solution.py:31
  39.0 8.6 %collective-permute-start.14 = (bf16[320,256]{1,0:T(8,128)(2,1)S(1)}, bf16[320,256]{1,0:T(8,128)(2,1)S(1)}, u32[]{:S(2)}, u32[]{:S(2)}) collective-permute-start(bf16[320,256]{1,0:T(8,128)(2,1)S(1)} %get-tuple-element.51), channel_id=1, source_target_pairs={{0,224},{1,225},{2,226},{3,227},{8,232},{9,233},{10,234},{11,235},... | collective-permute-start | bytes 491528 | tf_op jit(solution)/shard_map/reduce/ppermute | solution.py:31
  47.3 9.1 %collective-permute-start.11 = (bf16[576,256]{1,0:T(8,128)(2,1)S(1)}, bf16[576,256]{1,0:T(8,128)(2,1)S(1)}, u32[]{:S(2)}, u32[]{:S(2)}) collective-permute-start(bf16[576,256]{1,0:T(8,128)(2,1)S(1)} %pad_maximum_fusion), channel_id=1, source_target_pairs={{0,32},{1,33},{2,34},{3,35},{8,40},{9,41},{10,42},{11,43},{4,36},{... | collective-permute-start | bytes 884744 | tf_op jit(solution)/shard_map/reduce/ppermute | solution.py:31
  47.7 8.9 %collective-permute-start.15 = (bf16[576,256]{1,0:T(8,128)(2,1)S(1)}, bf16[576,256]{1,0:T(8,128)(2,1)S(1)}, u32[]{:S(2)}, u32[]{:S(2)}) collective-permute-start(bf16[576,256]{1,0:T(8,128)(2,1)S(1)} %pad_maximum_fusion.3), channel_id=1, source_target_pairs={{0,224},{1,225},{2,226},{3,227},{8,232},{9,233},{10,234},{11,235},... | collective-permute-start | bytes 884744 | tf_op jit(solution)/shard_map/reduce/ppermute | solution.py:31
  56.5 8.0 %collective-permute-start.12 = (bf16[576,256]{1,0:T(8,128)(2,1)S(1)}, bf16[576,256]{1,0:T(8,128)(2,1)S(1)}, u32[]{:S(2)}, u32[]{:S(2)}) collective-permute-start(bf16[576,256]{1,0:T(8,128)(2,1)S(1)} %pad_maximum_fusion.1), channel_id=1, source_target_pairs={{0,32},{1,33},{2,34},{3,35},{8,40},{9,41},{10,42},{11,43},{4,36},{... | collective-permute-start | bytes 884744 | tf_op jit(solution)/shard_map/reduce/ppermute | solution.py:31
  56.7 8.0 %collective-permute-start.16 = (bf16[576,256]{1,0:T(8,128)(2,1)S(1)}, bf16[576,256]{1,0:T(8,128)(2,1)S(1)}, u32[]{:S(2)}, u32[]{:S(2)}) collective-permute-start(bf16[576,256]{1,0:T(8,128)(2,1)S(1)} %pad_maximum_fusion.4), channel_id=1, source_target_pairs={{0,224},{1,225},{2,226},{3,227},{8,232},{9,233},{10,234},{11,235},... | collective-permute-start | bytes 884744 | tf_op jit(solution)/shard_map/reduce/ppermute | solution.py:31
  64.6 6.9 %collective-permute-start.13 = (bf16[576,256]{1,0:T(8,128)(2,1)S(1)}, bf16[576,256]{1,0:T(8,128)(2,1)S(1)}, u32[]{:S(2)}, u32[]{:S(2)}) collective-permute-start(bf16[576,256]{1,0:T(8,128)(2,1)S(1)} %pad_maximum_fusion.2), channel_id=1, source_target_pairs={{0,32},{1,33},{2,34},{3,35},{8,40},{9,41},{10,42},{11,43},{4,36},{... | collective-permute-start | bytes 884744 | tf_op jit(solution)/shard_map/reduce/ppermute | solution.py:31
  64.8 6.0 %collective-permute-start.17 = (bf16[512,256]{1,0:T(8,128)(2,1)S(1)}, bf16[512,256]{1,0:T(8,128)(2,1)S(1)}, u32[]{:S(2)}, u32[]{:S(2)}) collective-permute-start(bf16[512,256]{1,0:T(8,128)(2,1)S(1)} %add_convert_fusion), channel_id=1, source_target_pairs={{0,224},{1,225},{2,226},{3,227},{8,232},{9,233},{10,234},{11,235},... | collective-permute-start | bytes 786440 | tf_op jit(solution)/shard_map/reduce/ppermute | solution.py:31
  81.0 5.9 %collective-permute-start.23 = (bf16[256,256]{1,0:T(8,128)(2,1)S(1)}, bf16[256,256]{1,0:T(8,128)(2,1)S(1)}, u32[]{:S(2)}, u32[]{:S(2)}) collective-permute-start(bf16[256,256]{1,0:T(8,128)(2,1)S(1)} %collective-permute-done.22.refs_4_), channel_id=1, source_target_pairs={{0,32},{1,33},{2,34},{3,35},{8,40},{9,41},{10,42},{11,43},{4,36},{... | collective-permute-start | bytes 393224 | tf_op jit(solution)/shard_map/spread/ppermute | solution.py:31
  83.7 6.7 %collective-permute-start.30 = (bf16[256,256]{1,0:T(8,128)(2,1)S(1)}, bf16[256,256]{1,0:T(8,128)(2,1)S(1)}, u32[]{:S(2)}, u32[]{:S(2)}) collective-permute-start(bf16[256,256]{1,0:T(8,128)(2,1)S(1)} %collective-permute-done.29.refs_7_), channel_id=1, source_target_pairs={{0,32},{1,33},{2,34},{3,35},{8,40},{9,41},{10,42},{11,43},{4,36},{... | collective-permute-start | bytes 393224 | tf_op jit(solution)/shard_map/spread/ppermute | solution.py:31
  83.7 6.7 %collective-permute-start.20 = (bf16[256,256]{1,0:T(8,128)(2,1)S(1)}, bf16[256,256]{1,0:T(8,128)(2,1)S(1)}, u32[]{:S(2)}, u32[]{:S(2)}) collective-permute-start(bf16[256,256]{1,0:T(8,128)(2,1)S(1)} %collective-permute-done.19.refs_8_), channel_id=1, source_target_pairs={{0,224},{1,225},{2,226},{3,227},{8,232},{9,233},{10,234},{11,235},... | collective-permute-start | bytes 393224 | tf_op jit(solution)/shard_map/spread/ppermute | solution.py:31
  87.0 6.1 %collective-permute-start.24 = (bf16[256,256]{1,0:T(8,128)(2,1)S(1)}, bf16[256,256]{1,0:T(8,128)(2,1)S(1)}, u32[]{:S(2)}, u32[]{:S(2)}) collective-permute-start(bf16[256,256]{1,0:T(8,128)(2,1)S(1)} %collective-permute-done.23.refs_3_), channel_id=1, source_target_pairs={{0,32},{1,33},{2,34},{3,35},{8,40},{9,41},{10,42},{11,43},{4,36},{... | collective-permute-start | bytes 393224 | tf_op jit(solution)/shard_map/spread/ppermute | solution.py:31
  87.0 7.8 %collective-permute-start.28 = (bf16[256,256]{1,0:T(8,128)(2,1)S(1)}, bf16[256,256]{1,0:T(8,128)(2,1)S(1)}, u32[]{:S(2)}, u32[]{:S(2)}) collective-permute-start(bf16[256,256]{1,0:T(8,128)(2,1)S(1)} %collective-permute-done.27.refs_4_), channel_id=1, source_target_pairs={{0,224},{1,225},{2,226},{3,227},{8,232},{9,233},{10,234},{11,235},... | collective-permute-start | bytes 393224 | tf_op jit(solution)/shard_map/spread/ppermute | solution.py:31
  90.4 7.8 %collective-permute-start.21 = (bf16[256,256]{1,0:T(8,128)(2,1)S(1)}, bf16[256,256]{1,0:T(8,128)(2,1)S(1)}, u32[]{:S(2)}, u32[]{:S(2)}) collective-permute-start(bf16[256,256]{1,0:T(8,128)(2,1)S(1)} %collective-permute-done.20.refs_10_), channel_id=1, source_target_pairs={{0,224},{1,225},{2,226},{3,227},{8,232},{9,233},{10,234},{11,235},... | collective-permute-start | bytes 393224 | tf_op jit(solution)/shard_map/spread/ppermute | solution.py:31
  99.5 10.4 %collective-permute-start.33 = (f32[528,256]{1,0:T(8,128)S(1)}, f32[528,256]{1,0:T(8,128)S(1)}, u32[]{:S(2)}, u32[]{:S(2)}) collective-permute-start(f32[528,256]{1,0:T(8,128)S(1)} %get-tuple-element.63), channel_id=1, source_target_pairs={{0,16},{1,17},{2,18},{3,19},{8,24},{9,25},{10,26},{11,27},{4,20},{... | collective-permute-start | bytes 1622024 | tf_op jit(solution)/shard_map/direct/ppermute | solution.py:31
  110.0 9.5 %collective-permute-start.34 = (bf16[544,256]{1,0:T(8,128)(2,1)S(1)}, bf16[544,256]{1,0:T(8,128)(2,1)S(1)}, u32[]{:S(2)}, u32[]{:S(2)}) collective-permute-start(bf16[544,256]{1,0:T(8,128)(2,1)S(1)} %pad_maximum_fusion.5), channel_id=1, source_target_pairs={{0,4},{1,5},{2,6},{3,7},{8,12},{9,13},{10,14},{11,15},{4,0},{5,1},... | collective-permute-start | bytes 835592 | tf_op jit(solution)/shard_map/direct/ppermute | solution.py:31
  (13 other events, 61.3 us)

commit v4 on v3

--- a/solution.py
+++ b/solution.py
@@ -222,7 +222,9 @@
     return part - means[...] * totals[0:1, lanes]
 
 
-def far_kernel(place, means, totals, halves, other, packed, top, bottom):
+def far_kernel(place, own_sums, other_sums, halves, other, *outs):
+    top, bottom, packed, totals, means = outs
+    pack_kernel(2 * other.shape[1], place, own_sums, other_sums, packed, totals, means)
     index = lax.rem(place[0] + 4, NZ)
     value = centered(means, totals, halves, other, index).astype(BF)
     top[:BLK] = value[:BLK]
@@ -267,7 +269,7 @@
     bottom[...] = (value[BLK:] * column_scale).astype(BF)
 
 
-def reduce_rows(place, rows, means, totals, blocks, packed):
+def reduce_rows(place, rows, sums, blocks):
     height = 2 * BLK
     flops = 2 * rows.shape[0] * rows.shape[1] * BLK
     (halves,) = call(
@@ -281,8 +283,8 @@
         nbytes=6 << 20,
     )
 
-    def products(kernel, extra, count, shapes):
-        operands = [means, totals, halves, blocks[1], *extra]
+    def products(kernel, figures, count, shapes):
+        operands = [*figures, halves, blocks[1]]
         return call(
             kernel,
             "products",
@@ -296,9 +298,11 @@
 
     def wide(*offsets):
         kernel = functools.partial(product_kernel, offsets)
-        return products(kernel, (), len(offsets), [((height, BLK), F32)] * len(offsets))
-
-    top, bottom = products(far_kernel, [packed], 1, [((BLK + PACK, BLK), BF)] * 2)
+        return products(kernel, (means, totals), len(offsets), [((height, BLK), F32)] * len(offsets))
+
+    shapes = [((BLK + PACK, BLK), BF)] * 2
+    shapes += [((PACK, BLK), BF), ((2, 10 * BLK), F32), ((height, BLK), F32)]
+    top, bottom, packed, totals, means = products(far_kernel, sums, 1, shapes)
     from_left, from_right = z_shift(top, 1), z_shift(bottom, -1)
     gathered = [from_left, from_right]
     ahead, behind = wide(3, -3)
@@ -319,7 +323,7 @@
             left = [add(behind, from_right[:height]), from_right[height:]]
             if hop == 1:
                 left = left[:1]
-    return own, from_left, from_right, gathered[:-1]
+    return own, from_left, from_right, [packed, *gathered[:-1]]
 
 
 def gradient(place, own, from_left, from_right, packed, clip_total):
@@ -458,23 +462,16 @@
 
     with jax.named_scope("statistics"):
         own_sums, other_sums = column_sums(place, keep, send, student)
-        packed, totals, means = call(
-            functools.partial(pack_kernel, 2 * clips),
-            "pack",
-            place,
-            [own_sums, core_swap(other_sums)],
-            [None] * 2,
-            [((PACK, BLK), BF), ((2, 10 * BLK), F32), ((2 * BLK, BLK), F32)],
-        )
+        sums = own_sums, core_swap(other_sums)
 
     with jax.named_scope("reduce"):
         own, right, left, gathered = reduce_rows(
-            place, rows, means, totals, blocks, packed
+            place, rows, sums, blocks
         )
 
     with jax.named_scope("gradient"):
         top, bottom, sums, squares = gradient(
-            place, own, right, left, [packed, *gathered], clip_total
+            place, own, right, left, gathered, clip_total
         )
 
     with jax.named_scope("spread"):

time: 121 us -> 120 us (level)
    pallas_call x13 -> x12, Pallas kernels: 16.1 us -> 15.4 us  [call(): pl.pallas_call(body, grid_spec=pltpu.PrefetchScalarGridSpec(num_scalar_pr...]
  transfers between devices with their start and end apart: 35 -> 35, of which waited for: 16 -> 16; matrix products, arithmetic and copies ran while one was open for 1% -> 1% of each run, Pallas kernels for 9% -> 8%
where the time goes in v4:
time: 120 us
  starting transfers between devices  58.8 us (49%)
  waiting for transfers between devices  41.8 us (35%)
  Pallas kernels  15.4 us (13%)
  other arithmetic  1.69 us (1%)
  local copies, waits for them, and re-layouts  1.65 us (1%)
    ppermute x35, starting transfers between devices, move(): return lax.ppermute(value, ('batch', 'fi', 'fj'), pairs)  58.8 us
    ppermute x35, waiting for transfers between devices, move(): return lax.ppermute(value, ('batch', 'fi', 'fj'), pairs)  41.8 us
    pallas_call x12, Pallas kernels, call(): pl.pallas_call(body, grid_spec=pltpu.PrefetchScalarGridSpec(num_scalar_pr...  15.4 us
  transfers between devices with their start and end apart: 35, of which 16 were waited for; matrix products, arithmetic and copies ran while one was open for 1% of the time, Pallas kernels for 8%

profile of v4, /device:TPU:1, one launch (start us, length us, event | category | flops | bytes accessed | tf_op | source)
XLA Modules:
  0.0 119.7 jit_solution(12242611472959183934)
XLA Ops:
  2.3 3.4 %collective-permute-start = (bf16[512,1024]{1,0:T(8,128)(2,1)S(1)}, bf16[512,1024]{1,0:T(8,128)(2,1)S(1)}, u32[]{:S(2)}, u32[]{:S(2)}) collective-permute-start(bf16[512,1024]{1,0:T(8,128)(2,1)S(1)} %far_half.1), channel_id=1, source_target_pairs={{0,12},{1,13},{2,14},{3,15},{8,4},{9,5},{10,6},{11,7},{4,8},{5,9},... | collective-permute-start | bytes 3145736 | tf_op jit(solution)/shard_map/operand_blocks/ppermute | solution.py:31
  5.7 2.9 %collective-permute-start.2 = (bf16[512,256]{1,0:T(8,128)(2,1)S(1)}, bf16[512,256]{1,0:T(8,128)(2,1)S(1)}, u32[]{:S(2)}, u32[]{:S(2)}) collective-permute-start(bf16[512,256]{1,0:T(8,128)(2,1)S(1)} %copy-done.1), channel_id=1, source_target_pairs={{0,2},{1,3},{2,0},{3,1},{8,10},{9,11},{10,8},{11,9},{4,6},{5,7},{6... | collective-permute-start | bytes 786440 | tf_op jit(solution)/shard_map/operand_blocks/ppermute | solution.py:31
  10.1 2.5 %collective-permute-done.4.refs_8_ = bf16[512,256]{1,0:T(8,128)(2,1)S(1)} collective-permute-done((bf16[512,256]{1,0:T(8,128)(2,1)S(1)}, bf16[512,256]{1,0:T(8,128)(2,1)S(1)}, u32[]{:S(2)}, u32[]{:S(2)}) %collective-permute-start.4) | collective-permute-done | bytes 262176 | tf_op jit(solution)/shard_map/operand_blocks/ppermute | solution.py:31
  12.5 2.7 %collective-permute-start.5 = (bf16[512,256]{1,0:T(8,128)(2,1)S(1)}, bf16[512,256]{1,0:T(8,128)(2,1)S(1)}, u32[]{:S(2)}, u32[]{:S(2)}) collective-permute-start(bf16[512,256]{1,0:T(8,128)(2,1)S(1)} %collective-permute-done.4.refs_8_), channel_id=1, source_target_pairs={{0,3},{1,0},{2,1},{3,2},{8,11},{9,8},{10,9},{11,10},{4,7},{5,4},{6... | collective-permute-start | bytes 786440 | tf_op jit(solution)/shard_map/operand_blocks/ppermute | solution.py:31
  15.3 5.1 %collective-permute-done.1.refs_5_ = bf16[512,256]{1,0:T(8,128)(2,1)S(1)} collective-permute-done((bf16[512,256]{1,0:T(8,128)(2,1)S(1)}, bf16[512,256]{1,0:T(8,128)(2,1)S(1)}, u32[]{:S(2)}, u32[]{:S(2)}) %collective-permute-start.1) | collective-permute-done | bytes 262176 | tf_op jit(solution)/shard_map/operand_blocks/ppermute | solution.py:31
  22.6 3.4 %collective-permute-done.5.refs_9_ = bf16[512,256]{1,0:T(8,128)(2,1)S(1)} collective-permute-done((bf16[512,256]{1,0:T(8,128)(2,1)S(1)}, bf16[512,256]{1,0:T(8,128)(2,1)S(1)}, u32[]{:S(2)}, u32[]{:S(2)}) %collective-permute-start.5) | collective-permute-done | bytes 262176 | tf_op jit(solution)/shard_map/operand_blocks/ppermute | solution.py:31
  28.5 2.6 %collective-permute-start.9 = (bf16[10,512,256]{2,1,0:T(8,128)(2,1)S(1)}, bf16[10,512,256]{2,1,0:T(8,128)(2,1)S(1)}, u32[]{:S(2)}, u32[]{:S(2)}) collective-permute-start(bf16[10,512,256]{2,1,0:T(8,128)(2,1)S(1)} %get-tuple-element.37.refs_2_), channel_id=1, source_target_pairs={{0,16},{1,17},{2,18},{3,19},{8,24},{9,25},{10,26},{11,27},{4,20},{... | collective-permute-start | bytes 7864328 | tf_op jit(solution)/shard_map/stage/ppermute | solution.py:31
  38.2 4.0 %collective-permute-start.14 = (bf16[320,256]{1,0:T(8,128)(2,1)S(1)}, bf16[320,256]{1,0:T(8,128)(2,1)S(1)}, u32[]{:S(2)}, u32[]{:S(2)}) collective-permute-start(bf16[320,256]{1,0:T(8,128)(2,1)S(1)} %get-tuple-element.50), channel_id=1, source_target_pairs={{0,224},{1,225},{2,226},{3,227},{8,232},{9,233},{10,234},{11,235},... | collective-permute-start | bytes 491528 | tf_op jit(solution)/shard_map/reduce/ppermute | solution.py:31
  46.9 2.7 %collective-permute-start.15 = (bf16[576,256]{1,0:T(8,128)(2,1)S(1)}, bf16[576,256]{1,0:T(8,128)(2,1)S(1)}, u32[]{:S(2)}, u32[]{:S(2)}) collective-permute-start(bf16[576,256]{1,0:T(8,128)(2,1)S(1)} %pad_maximum_fusion.3), channel_id=1, source_target_pairs={{0,224},{1,225},{2,226},{3,227},{8,232},{9,233},{10,234},{11,235},... | collective-permute-start | bytes 884744 | tf_op jit(solution)/shard_map/reduce/ppermute | solution.py:31
  49.6 6.0 %collective-permute-done.11.refs_7_ = bf16[576,256]{1,0:T(8,128)(2,1)S(1)} collective-permute-done((bf16[576,256]{1,0:T(8,128)(2,1)S(1)}, bf16[576,256]{1,0:T(8,128)(2,1)S(1)}, u32[]{:S(2)}, u32[]{:S(2)}) %collective-permute-start.11) | collective-permute-done | bytes 294944 | tf_op jit(solution)/shard_map/reduce/ppermute | solution.py:31
  55.9 2.7 %collective-permute-start.16 = (bf16[576,256]{1,0:T(8,128)(2,1)S(1)}, bf16[576,256]{1,0:T(8,128)(2,1)S(1)}, u32[]{:S(2)}, u32[]{:S(2)}) collective-permute-start(bf16[576,256]{1,0:T(8,128)(2,1)S(1)} %pad_maximum_fusion.4), channel_id=1, source_target_pairs={{0,224},{1,225},{2,226},{3,227},{8,232},{9,233},{10,234},{11,235},... | collective-permute-start | bytes 884744 | tf_op jit(solution)/shard_map/reduce/ppermute | solution.py:31
  58.7 5.1 %collective-permute-done.12.refs_9_ = bf16[576,256]{1,0:T(8,128)(2,1)S(1)} collective-permute-done((bf16[576,256]{1,0:T(8,128)(2,1)S(1)}, bf16[576,256]{1,0:T(8,128)(2,1)S(1)}, u32[]{:S(2)}, u32[]{:S(2)}) %collective-permute-start.12) | collective-permute-done | bytes 294944 | tf_op jit(solution)/shard_map/reduce/ppermute | solution.py:31
  64.0 2.7 %collective-permute-start.17 = (bf16[512,256]{1,0:T(8,128)(2,1)S(1)}, bf16[512,256]{1,0:T(8,128)(2,1)S(1)}, u32[]{:S(2)}, u32[]{:S(2)}) collective-permute-start(bf16[512,256]{1,0:T(8,128)(2,1)S(1)} %add_convert_fusion), channel_id=1, source_target_pairs={{0,224},{1,225},{2,226},{3,227},{8,232},{9,233},{10,234},{11,235},... | collective-permute-start | bytes 786440 | tf_op jit(solution)/shard_map/reduce/ppermute | solution.py:31
  66.7 3.3 %collective-permute-done.17.refs_3_ = bf16[512,256]{1,0:T(8,128)(2,1)S(1)} collective-permute-done((bf16[512,256]{1,0:T(8,128)(2,1)S(1)}, bf16[512,256]{1,0:T(8,128)(2,1)S(1)}, u32[]{:S(2)}, u32[]{:S(2)}) %collective-permute-start.17) | collective-permute-done | bytes 262176 | tf_op jit(solution)/shard_map/reduce/ppermute | solution.py:31
  72.3 2.6 %collective-permute-start.18 = (bf16[256,256]{1,0:T(8,128)(2,1)S(1)}, bf16[256,256]{1,0:T(8,128)(2,1)S(1)}, u32[]{:S(2)}, u32[]{:S(2)}) collective-permute-start(bf16[256,256]{1,0:T(8,128)(2,1)S(1)} %get-tuple-element.54.refs_6_), channel_id=1, source_target_pairs={{0,224},{1,225},{2,226},{3,227},{8,232},{9,233},{10,234},{11,235},... | collective-permute-start | bytes 393224 | tf_op jit(solution)/shard_map/spread/ppermute | solution.py:31
  74.9 2.7 %collective-permute-start.26 = (bf16[256,256]{1,0:T(8,128)(2,1)S(1)}, bf16[256,256]{1,0:T(8,128)(2,1)S(1)}, u32[]{:S(2)}, u32[]{:S(2)}) collective-permute-start(bf16[256,256]{1,0:T(8,128)(2,1)S(1)} %get-tuple-element.55.refs_3_), channel_id=1, source_target_pairs={{0,224},{1,225},{2,226},{3,227},{8,232},{9,233},{10,234},{11,235},... | collective-permute-start | bytes 393224 | tf_op jit(solution)/shard_map/spread/ppermute | solution.py:31
  77.5 2.7 %collective-permute-start.19 = (bf16[256,256]{1,0:T(8,128)(2,1)S(1)}, bf16[256,256]{1,0:T(8,128)(2,1)S(1)}, u32[]{:S(2)}, u32[]{:S(2)}) collective-permute-start(bf16[256,256]{1,0:T(8,128)(2,1)S(1)} %collective-permute-done.18.refs_8_), channel_id=1, source_target_pairs={{0,224},{1,225},{2,226},{3,227},{8,232},{9,233},{10,234},{11,235},... | collective-permute-start | bytes 393224 | tf_op jit(solution)/shard_map/spread/ppermute | solution.py:31
  80.2 2.7 %collective-permute-start.27 = (bf16[256,256]{1,0:T(8,128)(2,1)S(1)}, bf16[256,256]{1,0:T(8,128)(2,1)S(1)}, u32[]{:S(2)}, u32[]{:S(2)}) collective-permute-start(bf16[256,256]{1,0:T(8,128)(2,1)S(1)} %collective-permute-done.26.refs_5_), channel_id=1, source_target_pairs={{0,224},{1,225},{2,226},{3,227},{8,232},{9,233},{10,234},{11,235},... | collective-permute-start | bytes 393224 | tf_op jit(solution)/shard_map/spread/ppermute | solution.py:31
  82.9 3.0 %collective-permute-start.20 = (bf16[256,256]{1,0:T(8,128)(2,1)S(1)}, bf16[256,256]{1,0:T(8,128)(2,1)S(1)}, u32[]{:S(2)}, u32[]{:S(2)}) collective-permute-start(bf16[256,256]{1,0:T(8,128)(2,1)S(1)} %collective-permute-done.19.refs_8_), channel_id=1, source_target_pairs={{0,224},{1,225},{2,226},{3,227},{8,232},{9,233},{10,234},{11,235},... | collective-permute-start | bytes 393224 | tf_op jit(solution)/shard_map/spread/ppermute | solution.py:31
  86.2 3.0 %collective-permute-start.28 = (bf16[256,256]{1,0:T(8,128)(2,1)S(1)}, bf16[256,256]{1,0:T(8,128)(2,1)S(1)}, u32[]{:S(2)}, u32[]{:S(2)}) collective-permute-start(bf16[256,256]{1,0:T(8,128)(2,1)S(1)} %collective-permute-done.27.refs_4_), channel_id=1, source_target_pairs={{0,224},{1,225},{2,226},{3,227},{8,232},{9,233},{10,234},{11,235},... | collective-permute-start | bytes 393224 | tf_op jit(solution)/shard_map/spread/ppermute | solution.py:31
  89.6 2.7 %collective-permute-start.21 = (bf16[256,256]{1,0:T(8,128)(2,1)S(1)}, bf16[256,256]{1,0:T(8,128)(2,1)S(1)}, u32[]{:S(2)}, u32[]{:S(2)}) collective-permute-start(bf16[256,256]{1,0:T(8,128)(2,1)S(1)} %collective-permute-done.20.refs_10_), channel_id=1, source_target_pairs={{0,224},{1,225},{2,226},{3,227},{8,232},{9,233},{10,234},{11,235},... | collective-permute-start | bytes 393224 | tf_op jit(solution)/shard_map/spread/ppermute | solution.py:31
  95.4 1.9 %direct_part.4 = (f32[1040,512]{1,0:T(8,128)S(1)}, f32[256,512]{1,0:T(8,128)S(1)}) custom-call(s32[4]{0:T(128)S(1)} %pad_add_fusion.refs_0_, bf16[8,512,256]{2,1,0:T(8,128)(2,1)S(1)} %get-tuple-element.36.refs_1_.refs_2_, bf16[10,512,256]{2,1,0:T(8,128)(2,1)S(1)} %collective-permute-done.9.refs_4_.refs_2_, ...), custom_call_target="tpu_custom_call" | custom-call | flops 1073741824 | bytes 2097152 | tf_op jit(solution)/shard_map/direct/direct_part/pallas_call | solution.py:80
  98.7 8.8 %collective-permute-start.33 = (f32[528,256]{1,0:T(8,128)S(1)}, f32[528,256]{1,0:T(8,128)S(1)}, u32[]{:S(2)}, u32[]{:S(2)}) collective-permute-start(f32[528,256]{1,0:T(8,128)S(1)} %get-tuple-element.63), channel_id=1, source_target_pairs={{0,16},{1,17},{2,18},{3,19},{8,24},{9,25},{10,26},{11,27},{4,20},{... | collective-permute-start | bytes 1622024 | tf_op jit(solution)/shard_map/direct/ppermute | solution.py:31
  110.9 7.7 %collective-permute-done.34 = bf16[544,256]{1,0:T(8,128)(2,1)S(1)} collective-permute-done((bf16[544,256]{1,0:T(8,128)(2,1)S(1)}, bf16[544,256]{1,0:T(8,128)(2,1)S(1)}, u32[]{:S(2)}, u32[]{:S(2)}) %collective-permute-start.34) | collective-permute-done | bytes 278560 | tf_op jit(solution)/shard_map/direct/ppermute | solution.py:31
  (91 shorter events, 32.4 us)
Async XLA Ops:
  2.3 25.2 %collective-permute-start = (bf16[512,1024]{1,0:T(8,128)(2,1)S(1)}, bf16[512,1024]{1,0:T(8,128)(2,1)S(1)}, u32[]{:S(2)}, u32[]{:S(2)}) collective-permute-start(bf16[512,1024]{1,0:T(8,128)(2,1)S(1)} %far_half.1), channel_id=1, source_target_pairs={{0,12},{1,13},{2,14},{3,15},{8,4},{9,5},{10,6},{11,7},{4,8},{5,9},... | collective-permute-start | bytes 3145736 | tf_op jit(solution)/shard_map/operand_blocks/ppermute | solution.py:31
  5.7 6.9 %collective-permute-start.4 = (bf16[512,256]{1,0:T(8,128)(2,1)S(1)}, bf16[512,256]{1,0:T(8,128)(2,1)S(1)}, u32[]{:S(2)}, u32[]{:S(2)}) collective-permute-start(bf16[512,256]{1,0:T(8,128)(2,1)S(1)} %copy-done.1), channel_id=1, source_target_pairs={{0,8},{1,9},{2,10},{3,11},{8,0},{9,1},{10,2},{11,3},{4,12},{5,13},... | collective-permute-start | bytes 786440 | tf_op jit(solution)/shard_map/operand_blocks/ppermute | solution.py:31
  5.7 9.6 %collective-permute-start.2 = (bf16[512,256]{1,0:T(8,128)(2,1)S(1)}, bf16[512,256]{1,0:T(8,128)(2,1)S(1)}, u32[]{:S(2)}, u32[]{:S(2)}) collective-permute-start(bf16[512,256]{1,0:T(8,128)(2,1)S(1)} %copy-done.1), channel_id=1, source_target_pairs={{0,2},{1,3},{2,0},{3,1},{8,10},{9,11},{10,8},{11,9},{4,6},{5,7},{6... | collective-permute-start | bytes 786440 | tf_op jit(solution)/shard_map/operand_blocks/ppermute | solution.py:31
  8.6 11.8 %collective-permute-start.1 = (bf16[512,256]{1,0:T(8,128)(2,1)S(1)}, bf16[512,256]{1,0:T(8,128)(2,1)S(1)}, u32[]{:S(2)}, u32[]{:S(2)}) collective-permute-start(bf16[512,256]{1,0:T(8,128)(2,1)S(1)} %copy-done.1), channel_id=1, source_target_pairs={{0,3},{1,0},{2,1},{3,2},{8,11},{9,8},{10,9},{11,10},{4,7},{5,4},{6... | collective-permute-start | bytes 786440 | tf_op jit(solution)/shard_map/operand_blocks/ppermute | solution.py:31
  9.4 13.2 %collective-permute-start.3 = (bf16[512,256]{1,0:T(8,128)(2,1)S(1)}, bf16[512,256]{1,0:T(8,128)(2,1)S(1)}, u32[]{:S(2)}, u32[]{:S(2)}) collective-permute-start(bf16[512,256]{1,0:T(8,128)(2,1)S(1)} %copy-done.1), channel_id=1, source_target_pairs={{0,1},{1,2},{2,3},{3,0},{8,9},{9,10},{10,11},{11,8},{4,5},{5,6},{6... | collective-permute-start | bytes 786440 | tf_op jit(solution)/shard_map/operand_blocks/ppermute | solution.py:31
  12.5 13.4 %collective-permute-start.5 = (bf16[512,256]{1,0:T(8,128)(2,1)S(1)}, bf16[512,256]{1,0:T(8,128)(2,1)S(1)}, u32[]{:S(2)}, u32[]{:S(2)}) collective-permute-start(bf16[512,256]{1,0:T(8,128)(2,1)S(1)} %collective-permute-done.4.refs_8_), channel_id=1, source_target_pairs={{0,3},{1,0},{2,1},{3,2},{8,11},{9,8},{10,9},{11,10},{4,7},{5,4},{6... | collective-permute-start | bytes 786440 | tf_op jit(solution)/shard_map/operand_blocks/ppermute | solution.py:31
  15.3 10.7 %collective-permute-start.7 = (bf16[512,256]{1,0:T(8,128)(2,1)S(1)}, bf16[512,256]{1,0:T(8,128)(2,1)S(1)}, u32[]{:S(2)}, u32[]{:S(2)}) collective-permute-start(bf16[512,256]{1,0:T(8,128)(2,1)S(1)} %collective-permute-done.4.refs_8_), channel_id=1, source_target_pairs={{0,1},{1,2},{2,3},{3,0},{8,9},{9,10},{10,11},{11,8},{4,5},{5,6},{6... | collective-permute-start | bytes 786440 | tf_op jit(solution)/shard_map/operand_blocks/ppermute | solution.py:31
  28.5 7.1 %collective-permute-start.9 = (bf16[10,512,256]{2,1,0:T(8,128)(2,1)S(1)}, bf16[10,512,256]{2,1,0:T(8,128)(2,1)S(1)}, u32[]{:S(2)}, u32[]{:S(2)}) collective-permute-start(bf16[10,512,256]{2,1,0:T(8,128)(2,1)S(1)} %get-tuple-element.37.refs_2_), channel_id=1, source_target_pairs={{0,16},{1,17},{2,18},{3,19},{8,24},{9,25},{10,26},{11,27},{4,20},{... | collective-permute-start | bytes 7864328 | tf_op jit(solution)/shard_map/stage/ppermute | solution.py:31
  36.5 9.9 %collective-permute-start.10 = (bf16[320,256]{1,0:T(8,128)(2,1)S(1)}, bf16[320,256]{1,0:T(8,128)(2,1)S(1)}, u32[]{:S(2)}, u32[]{:S(2)}) collective-permute-start(bf16[320,256]{1,0:T(8,128)(2,1)S(1)} %get-tuple-element.46), channel_id=1, source_target_pairs={{0,32},{1,33},{2,34},{3,35},{8,40},{9,41},{10,42},{11,43},{4,36},{... | collective-permute-start | bytes 491528 | tf_op jit(solution)/shard_map/reduce/ppermute | solution.py:31
  38.2 8.5 %collective-permute-start.14 = (bf16[320,256]{1,0:T(8,128)(2,1)S(1)}, bf16[320,256]{1,0:T(8,128)(2,1)S(1)}, u32[]{:S(2)}, u32[]{:S(2)}) collective-permute-start(bf16[320,256]{1,0:T(8,128)(2,1)S(1)} %get-tuple-element.50), channel_id=1, source_target_pairs={{0,224},{1,225},{2,226},{3,227},{8,232},{9,233},{10,234},{11,235},... | collective-permute-start | bytes 491528 | tf_op jit(solution)/shard_map/reduce/ppermute | solution.py:31
  46.5 9.1 %collective-permute-start.11 = (bf16[576,256]{1,0:T(8,128)(2,1)S(1)}, bf16[576,256]{1,0:T(8,128)(2,1)S(1)}, u32[]{:S(2)}, u32[]{:S(2)}) collective-permute-start(bf16[576,256]{1,0:T(8,128)(2,1)S(1)} %pad_maximum_fusion), channel_id=1, source_target_pairs={{0,32},{1,33},{2,34},{3,35},{8,40},{9,41},{10,42},{11,43},{4,36},{... | collective-permute-start | bytes 884744 | tf_op jit(solution)/shard_map/reduce/ppermute | solution.py:31
  46.9 8.9 %collective-permute-start.15 = (bf16[576,256]{1,0:T(8,128)(2,1)S(1)}, bf16[576,256]{1,0:T(8,128)(2,1)S(1)}, u32[]{:S(2)}, u32[]{:S(2)}) collective-permute-start(bf16[576,256]{1,0:T(8,128)(2,1)S(1)} %pad_maximum_fusion.3), channel_id=1, source_target_pairs={{0,224},{1,225},{2,226},{3,227},{8,232},{9,233},{10,234},{11,235},... | collective-permute-start | bytes 884744 | tf_op jit(solution)/shard_map/reduce/ppermute | solution.py:31
  55.7 8.0 %collective-permute-start.12 = (bf16[576,256]{1,0:T(8,128)(2,1)S(1)}, bf16[576,256]{1,0:T(8,128)(2,1)S(1)}, u32[]{:S(2)}, u32[]{:S(2)}) collective-permute-start(bf16[576,256]{1,0:T(8,128)(2,1)S(1)} %pad_maximum_fusion.1), channel_id=1, source_target_pairs={{0,32},{1,33},{2,34},{3,35},{8,40},{9,41},{10,42},{11,43},{4,36},{... | collective-permute-start | bytes 884744 | tf_op jit(solution)/shard_map/reduce/ppermute | solution.py:31
  55.9 8.0 %collective-permute-start.16 = (bf16[576,256]{1,0:T(8,128)(2,1)S(1)}, bf16[576,256]{1,0:T(8,128)(2,1)S(1)}, u32[]{:S(2)}, u32[]{:S(2)}) collective-permute-start(bf16[576,256]{1,0:T(8,128)(2,1)S(1)} %pad_maximum_fusion.4), channel_id=1, source_target_pairs={{0,224},{1,225},{2,226},{3,227},{8,232},{9,233},{10,234},{11,235},... | collective-permute-start | bytes 884744 | tf_op jit(solution)/shard_map/reduce/ppermute | solution.py:31
  63.8 6.9 %collective-permute-start.13 = (bf16[576,256]{1,0:T(8,128)(2,1)S(1)}, bf16[576,256]{1,0:T(8,128)(2,1)S(1)}, u32[]{:S(2)}, u32[]{:S(2)}) collective-permute-start(bf16[576,256]{1,0:T(8,128)(2,1)S(1)} %pad_maximum_fusion.2), channel_id=1, source_target_pairs={{0,32},{1,33},{2,34},{3,35},{8,40},{9,41},{10,42},{11,43},{4,36},{... | collective-permute-start | bytes 884744 | tf_op jit(solution)/shard_map/reduce/ppermute | solution.py:31
  64.0 6.0 %collective-permute-start.17 = (bf16[512,256]{1,0:T(8,128)(2,1)S(1)}, bf16[512,256]{1,0:T(8,128)(2,1)S(1)}, u32[]{:S(2)}, u32[]{:S(2)}) collective-permute-start(bf16[512,256]{1,0:T(8,128)(2,1)S(1)} %add_convert_fusion), channel_id=1, source_target_pairs={{0,224},{1,225},{2,226},{3,227},{8,232},{9,233},{10,234},{11,235},... | collective-permute-start | bytes 786440 | tf_op jit(solution)/shard_map/reduce/ppermute | solution.py:31
  80.2 5.9 %collective-permute-start.23 = (bf16[256,256]{1,0:T(8,128)(2,1)S(1)}, bf16[256,256]{1,0:T(8,128)(2,1)S(1)}, u32[]{:S(2)}, u32[]{:S(2)}) collective-permute-start(bf16[256,256]{1,0:T(8,128)(2,1)S(1)} %collective-permute-done.22.refs_4_), channel_id=1, source_target_pairs={{0,32},{1,33},{2,34},{3,35},{8,40},{9,41},{10,42},{11,43},{4,36},{... | collective-permute-start | bytes 393224 | tf_op jit(solution)/shard_map/spread/ppermute | solution.py:31
  82.9 6.7 %collective-permute-start.30 = (bf16[256,256]{1,0:T(8,128)(2,1)S(1)}, bf16[256,256]{1,0:T(8,128)(2,1)S(1)}, u32[]{:S(2)}, u32[]{:S(2)}) collective-permute-start(bf16[256,256]{1,0:T(8,128)(2,1)S(1)} %collective-permute-done.29.refs_7_), channel_id=1, source_target_pairs={{0,32},{1,33},{2,34},{3,35},{8,40},{9,41},{10,42},{11,43},{4,36},{... | collective-permute-start | bytes 393224 | tf_op jit(solution)/shard_map/spread/ppermute | solution.py:31
  82.9 6.7 %collective-permute-start.20 = (bf16[256,256]{1,0:T(8,128)(2,1)S(1)}, bf16[256,256]{1,0:T(8,128)(2,1)S(1)}, u32[]{:S(2)}, u32[]{:S(2)}) collective-permute-start(bf16[256,256]{1,0:T(8,128)(2,1)S(1)} %collective-permute-done.19.refs_8_), channel_id=1, source_target_pairs={{0,224},{1,225},{2,226},{3,227},{8,232},{9,233},{10,234},{11,235},... | collective-permute-start | bytes 393224 | tf_op jit(solution)/shard_map/spread/ppermute | solution.py:31
  86.2 6.1 %collective-permute-start.24 = (bf16[256,256]{1,0:T(8,128)(2,1)S(1)}, bf16[256,256]{1,0:T(8,128)(2,1)S(1)}, u32[]{:S(2)}, u32[]{:S(2)}) collective-permute-start(bf16[256,256]{1,0:T(8,128)(2,1)S(1)} %collective-permute-done.23.refs_3_), channel_id=1, source_target_pairs={{0,32},{1,33},{2,34},{3,35},{8,40},{9,41},{10,42},{11,43},{4,36},{... | collective-permute-start | bytes 393224 | tf_op jit(solution)/shard_map/spread/ppermute | solution.py:31
  86.2 7.8 %collective-permute-start.28 = (bf16[256,256]{1,0:T(8,128)(2,1)S(1)}, bf16[256,256]{1,0:T(8,128)(2,1)S(1)}, u32[]{:S(2)}, u32[]{:S(2)}) collective-permute-start(bf16[256,256]{1,0:T(8,128)(2,1)S(1)} %collective-permute-done.27.refs_4_), channel_id=1, source_target_pairs={{0,224},{1,225},{2,226},{3,227},{8,232},{9,233},{10,234},{11,235},... | collective-permute-start | bytes 393224 | tf_op jit(solution)/shard_map/spread/ppermute | solution.py:31
  89.6 7.8 %collective-permute-start.21 = (bf16[256,256]{1,0:T(8,128)(2,1)S(1)}, bf16[256,256]{1,0:T(8,128)(2,1)S(1)}, u32[]{:S(2)}, u32[]{:S(2)}) collective-permute-start(bf16[256,256]{1,0:T(8,128)(2,1)S(1)} %collective-permute-done.20.refs_10_), channel_id=1, source_target_pairs={{0,224},{1,225},{2,226},{3,227},{8,232},{9,233},{10,234},{11,235},... | collective-permute-start | bytes 393224 | tf_op jit(solution)/shard_map/spread/ppermute | solution.py:31
  98.7 10.4 %collective-permute-start.33 = (f32[528,256]{1,0:T(8,128)S(1)}, f32[528,256]{1,0:T(8,128)S(1)}, u32[]{:S(2)}, u32[]{:S(2)}) collective-permute-start(f32[528,256]{1,0:T(8,128)S(1)} %get-tuple-element.63), channel_id=1, source_target_pairs={{0,16},{1,17},{2,18},{3,19},{8,24},{9,25},{10,26},{11,27},{4,20},{... | collective-permute-start | bytes 1622024 | tf_op jit(solution)/shard_map/direct/ppermute | solution.py:31
  109.2 9.5 %collective-permute-start.34 = (bf16[544,256]{1,0:T(8,128)(2,1)S(1)}, bf16[544,256]{1,0:T(8,128)(2,1)S(1)}, u32[]{:S(2)}, u32[]{:S(2)}) collective-permute-start(bf16[544,256]{1,0:T(8,128)(2,1)S(1)} %pad_maximum_fusion.5), channel_id=1, source_target_pairs={{0,4},{1,5},{2,6},{3,7},{8,12},{9,13},{10,14},{11,15},{4,0},{5,1},... | collective-permute-start | bytes 835592 | tf_op jit(solution)/shard_map/direct/ppermute | solution.py:31
  (13 other events, 61.3 us)
